TPU v7x, 256 devices: a whole 4x4x8 slice. The times are simulated.
256 devices in a mesh: tp: 32 (over y_hi, z, core), dp: 8 (over x, y_lo).
Axes of the slice: x: 4, y: 4 (y_hi: 2, y_lo: 2; y = y_hi * 2 + y_lo), z: 8, core: 2. Of those that a mesh axis runs over, the one named last changes fastest.
Arguments:
- teacher_hidden: bfloat16 [512, 16384], P('tp', 'dp'), may hold values from -6 to 6
- teacher_gain: bfloat16 [16384], P('dp'), may hold values from 0.5 to 1.5
- teacher_head: bfloat16 [16384, 65536], P('dp', 'tp'), as said below
- student_hidden: bfloat16 [512, 4096], P(('tp', 'dp')), may hold values from -6 to 6
- student_gain: bfloat16 [4096], replicated, may hold values from 0.5 to 1.5
- student_head: bfloat16 [4096, 65536], P(None, ('tp', 'dp')), as said below
- token_ids: int32 [512], replicated, may hold values from 0 to 65535
Outputs:
- token_loss: float32 [512], replicated
- grad_hidden: bfloat16 [512, 4096], P(('tp', 'dp'))
- grad_gain: float32 [4096], replicated
- grad_head: bfloat16 [4096, 65536], P(None, ('tp', 'dp'))
Inputs may be any that keep to these rules, and one draw needn't show every extreme that they name: `teacher_head`: entries of order 3 / sqrt(16384); some columns may be much larger. `student_head`: entries of order 3 / sqrt(4096); some columns may be much larger.
All inputs are finite; a program needn't handle non-finite values.
Results may differ from a plain program's by a relative error of at most 0.011.
Values may be sent and summed in bfloat16 or wider, within the bound.
A program may use at most 128 MiB of HBM per device.

v0:
```python
import jax
import jax.numpy as jnp
from jax import lax
from jax.sharding import PartitionSpec as P

D_T = 16384
D_S = 4096


epsilon = 1e-05
hard_weight = 0.5
loss_scale = 64.0


def shards(
    teacher_hidden,
    teacher_gain,
    teacher_head,
    student_hidden,
    student_gain,
    student_head,
    token_ids,
):
    gathered = lax.all_gather(teacher_hidden, "tp", axis=0, tiled=True)
    widened = gathered.astype(jnp.float32)
    square_total = lax.psum(jnp.sum(widened * widened, -1), "dp")
    teacher_inv = lax.rsqrt(square_total / D_T + epsilon)
    teacher_scaled = (widened * teacher_gain.astype(jnp.float32)).astype(jnp.bfloat16)
    partial_logits = jnp.dot(teacher_scaled, teacher_head, preferred_element_type=jnp.float32)
    columns_summed = lax.psum_scatter(partial_logits, "dp", scatter_dimension=1, tiled=True)
    teacher_logits = columns_summed * teacher_inv[:, None]
    full_rows = lax.all_gather(student_hidden, ("tp", "dp"), axis=0, tiled=True)
    student_wide = full_rows.astype(jnp.float32)
    student_inv = lax.rsqrt(jnp.sum(student_wide * student_wide, -1) / D_S + epsilon)
    gain_wide = student_gain.astype(jnp.float32)
    student_features = (student_wide * student_inv[:, None] * gain_wide).astype(jnp.bfloat16)
    student_logits = jnp.dot(student_features, student_head, preferred_element_type=jnp.float32)
    slice_width = student_head.shape[1]
    owner = lax.axis_index("tp") * lax.axis_size("dp") + lax.axis_index("dp")
    columns = owner * slice_width + jnp.arange(slice_width, dtype=jnp.int32)
    target_mask = columns[None, :] == token_ids[:, None]
    target_part = jnp.sum(jnp.where(target_mask, student_logits, 0.0), -1)
    logit_gap = teacher_logits - student_logits
    teacher_top, student_top = lax.pmax(
        (jnp.max(teacher_logits, -1), jnp.max(student_logits, -1)), ("tp", "dp")
    )
    teacher_exp = jnp.exp(teacher_logits - teacher_top[:, None])
    student_exp = jnp.exp(student_logits - student_top[:, None])
    teacher_total, student_total, cross_term, target = lax.psum(
        (
            jnp.sum(teacher_exp, -1),
            jnp.sum(student_exp, -1),
            jnp.sum(teacher_exp * logit_gap, -1),
            target_part,
        ),
        ("tp", "dp"),
    )
    teacher_lse = teacher_top + jnp.log(teacher_total)
    student_lse = student_top + jnp.log(student_total)
    token_loss = (
        cross_term / teacher_total
        - teacher_lse
        + student_lse
        + hard_weight * (student_lse - target)
    )
    teacher_prob = jnp.exp(teacher_logits - teacher_lse[:, None])
    student_prob = jnp.exp(student_logits - student_lse[:, None])
    onehot = target_mask.astype(jnp.float32)
    grad_logits = (
        loss_scale * (student_prob - teacher_prob + hard_weight * (student_prob - onehot))
    ).astype(jnp.bfloat16)
    grad_head = lax.dot_general(
        student_features, grad_logits, (((0,), (0,)), ((), ())), preferred_element_type=jnp.float32
    ).astype(jnp.bfloat16)
    grad_features = lax.psum_scatter(
        lax.dot_general(
            grad_logits, student_head, (((1,), (1,)), ((), ())), preferred_element_type=jnp.float32
        ),
        ("tp", "dp"),
        scatter_dimension=0,
        tiled=True,
    )
    own_wide = student_hidden.astype(jnp.float32)
    own_inv = lax.rsqrt(jnp.sum(own_wide * own_wide, -1) / D_S + epsilon)
    own_normed = own_wide * own_inv[:, None]
    grad_gain = lax.psum(jnp.sum(grad_features * own_normed, 0), ("tp", "dp"))
    grad_normed = grad_features * gain_wide
    inner = jnp.sum(grad_normed * own_normed, -1) / D_S
    grad_hidden = (own_inv[:, None] * (grad_normed - own_normed * inner[:, None])).astype(
        jnp.bfloat16
    )
    return (token_loss, grad_hidden, grad_gain, grad_head)


def solution(mesh):
    in_specs = (
        P("tp", "dp"),
        P("dp"),
        P("dp", "tp"),
        P(("tp", "dp"), None),
        P(),
        P(None, ("tp", "dp")),
        P(),
    )
    out_specs = (P(), P(("tp", "dp"), None), P(), P(None, ("tp", "dp")))
    return jax.shard_map(shards, mesh=mesh, in_specs=in_specs, out_specs=out_specs, check_vma=False)
```

profile of v0, /device:TPU:1, one launch (start us, length us, event | category | flops | bytes accessed | tf_op | source)
XLA Modules:
  0.0 1415.3 jit_solution(3035042727933590511)
XLA Ops:
  7.2 0.7 all-gather.4.cloned.1.call-update
  8.0 0.7 all-gather.6.cloned.1.call-update
  8.7 0.7 convert_element_type.34
  9.4 85.6 %all-gather.4.cloned.1.call-done = bf16[512,2048]{1,0:T(8,128)(2,1)} async-done(((bf16[16,2048]{1,0:T(8,128)(2,1)}), bf16[512,2048]{1,0:T(8,128)(2,1)}) %all-gather.4.cloned.1.call-update) | async-done | bytes 2097168 | tf_op jit(solution)/shard_map/all_gather | solution.py:24
  95.0 10.5 fusion.2
  106.2 2.1 fusion.1
  108.3 14.9 %psum.42 = f32[512]{0:T(512)S(1)} all-reduce(f32[512]{0:T(512)S(1)} %fusion.1), channel_id=1, replica_groups=mesh['tp'=32,'dp'=8] {'dp'}, use_global_device_ids=true, to_apply=%region_2.0 | all-reduce | flops 512 | bytes 4096 | tf_op jit(solution)/shard_map/psum | solution.py:26
  123.2 677.3 %all-gather.6.cloned.1.call-done = bf16[256,2,4096]{2,1,0:T(2,128)(2,1)} async-done(((bf16[1,2,4096]{2,1,0:T(2,128)(2,1)}), bf16[256,2,4096]{2,1,0:T(2,128)(2,1)}) %all-gather.6.cloned.1.call-update) | async-done | bytes 4194320 | tf_op jit(solution)/shard_map/all_gather | solution.py:32
  800.5 7.6 reshape.35
  808.1 4.2 multiply_reduce_fusion
  812.3 1.7 copy-done.1
  813.9 1.6 fusion.25
  815.8 79.3 %reduce-scatter.2.cloned.1.call-done = f32[512,256]{1,0:T(8,128)} async-done(((f32[512,2048]{1,0:T(8,128)}), f32[512,256]{1,0:T(8,128)}) %reduce-scatter.2.cloned.1.call-update) | async-done | bytes 524304 | tf_op jit(solution)/shard_map/reduce_scatter | solution.py:30
  895.0 1.3 multiply_reduce_fusion.2
  896.3 77.2 %all-reduce.3 = (f32[512]{0:T(512)S(1)}, f32[512]{0:T(512)S(1)}) all-reduce(f32[512]{0:T(512)S(1)} %get-tuple-element.16, f32[512]{0:T(512)S(1)} %multiply_reduce_fusion.2), channel_id=1, replica_groups=mesh['tp'=32,'dp'=8] {'tp','dp'}, use_global_device_ids=true, to_apply=%region_11.12 | all-reduce | flops 1024 | bytes 8192 | tf_op jit(solution)/shard_map/pmax | solution.py:44
  973.6 1.5 fusion.11
  975.2 73.5 %all-reduce.2 = (f32[512]{0:T(512)S(1)}, f32[512]{0:T(512)S(1)}) all-reduce(f32[512]{0:T(512)S(1)} %exponential_reduce_fusion, f32[512]{0:T(512)S(1)} %get-tuple-element.6), channel_id=1, replica_groups=mesh['tp'=32,'dp'=8] {'tp','dp'}, use_global_device_ids=true, to_apply=%region_13.14 | all-reduce | flops 1024 | bytes 8192 | tf_op jit(solution)/shard_map/psum | solution.py:49
  1048.7 5.7 fusion.23
  1054.4 0.7 copy-done.3
  1055.4 6.6 convolution_convert_fusion
  1062.0 265.7 %all-reduce.6.cloned.1.call-done = f32[512,4096]{1,0:T(8,128)} async-done(((f32[512,4096]{1,0:T(8,128)}), f32[512,4096]{1,0:T(8,128)}) %all-reduce.6.cloned.1.call-update) | async-done | bytes 8388624
  1327.7 1.1 fusion.18
  1328.9 77.7 %all-reduce.1 = (f32[512]{0:T(512)S(1)}, f32[512]{0:T(512)S(1)}, f32[4096]{0:T(1024)}) all-reduce(f32[512]{0:T(512)S(1)} %get-tuple-element.8, f32[512]{0:T(512)S(1)} %get-tuple-element.7, f32[4096]{0:T(1024)S(1)} %get-tuple-element.4), channel_id=1, replica_groups=mesh['tp'=32,'dp'=8] {'tp','dp'}, use_global_device_ids=true, to_apply=%region_15.16 | all-reduce | flops 5120 | bytes 40960 | tf_op jit(solution)/shard_map/psum | solution.py:49
  1407.2 1.6 fusion.20
  (27 shorter events, 2.1 us)
Async XLA Ops:
  7.2 805.1 %copy-start = (bf16[4096,256]{1,0:T(8,128)(2,1)S(1)}, bf16[4096,256]{1,0:T(8,128)(2,1)}, u32[]{:S(2)}) copy-start(bf16[4096,256]{1,0:T(8,128)(2,1)} %param.12) | copy-start | bytes 6291460
  7.2 87.8 %all-gather.4.cloned.1.call-start = ((), (), s32[]{:S(2)}) async-start(), calls=%async_computation.1 | async-start | bytes 2162688 | tf_op jit(solution)/shard_map/all_gather | solution.py:24
  7.9 792.6 %all-gather.6.cloned.1.call-start = ((), (), s32[]{:S(2)}) async-start(), calls=%async_computation.3 | async-start | bytes 4210688 | tf_op jit(solution)/shard_map/all_gather | solution.py:32
  8.7 886.4 %reduce-scatter.2.cloned.1.call-start = ((), (), s32[]{:S(2)}) async-start(), calls=%async_computation.2 | async-start | bytes 4718592 | tf_op jit(solution)/shard_map/reduce_scatter | solution.py:30
  105.5 0.7 copy-start.5
  105.5 1222.2 %all-reduce.6.cloned.1.call-start = ((), (), s32[]{:S(2)}) async-start(), calls=%async_computation.4 | async-start | bytes 16777216
  808.1 5.9 copy-start.1
  813.9 159.7 %copy-start.4 = (s32[512]{0:T(512)S(1)}, s32[512]{0:T(512)}, u32[]{:S(2)}) copy-start(s32[512]{0:T(512)} %param.13) | copy-start | bytes 6148
  1054.4 0.7 copy-start.3
  1054.4 1.1 copy-start.2
Sparse Core Ops, SparseCore 0:
  10.8 84.1 all-gather.3
  96.9 703.5 all-gather.5
  803.1 91.9 reduce-scatter.1
  1054.5 273.1 all-reduce.5
where the time goes:
time: 1420 us
  waiting for transfers between devices  1110 us (78%)
  blocking collectives  243 us (17%)
  matrix products  24.3 us (2%)
    all_gather x1, waiting for transfers between devices, shards(): full_rows = lax.all_gather(student_hidden, ('tp', 'dp'), axis=0, tiled=True)  677 us
    unnamed x5, waiting for transfers between devices  267 us
    psum x2, blocking collectives, shards(): lax.psum((jnp.sum(teacher_exp, -1), jnp.sum(student_exp, -1), jnp.sum(tea...  151 us
    all_gather x1, waiting for transfers between devices, shards(): gathered = lax.all_gather(teacher_hidden, 'tp', axis=0, tiled=True)  85.6 us
    reduce_scatter x1, waiting for transfers between devices, shards(): lax.psum_scatter(partial_logits, 'dp', scatter_dimension=1, tiled=True)  79.3 us
    pmax x1, blocking collectives, shards(): lax.pmax((jnp.max(teacher_logits, -1), jnp.max(student_logits, -1)), ('tp...  77.2 us
  transfers between devices with their start and end apart: 4, of which 4 were waited for; matrix products, arithmetic and copies ran while one was open for 2% of the time, Pallas kernels for 0%

commit v1 on v0

v1 whole, which is shorter than its diff:
```python
import functools

import jax
import jax.numpy as jnp
from jax import lax
from jax.experimental import pallas as pl
from jax.experimental.pallas import tpu as pltpu
from jax.sharding import PartitionSpec as P

D_T = 16384
D_S = 4096
TOKENS = 512
SLICE = 256

epsilon = 1e-05
hard_weight = 0.5
loss_scale = 64.0

MESH = pl.DeviceIdType.MESH
f32 = jnp.float32
bf16 = jnp.bfloat16
NT = (((1,), (1,)), ((), ()))

CHUNK_ROWS = (64, 128, 128, 128, 64)
CHUNK_AT = (0, 64, 192, 320, 448)
ORDER = (0, 2, 1, 3)
WIDE = 1024


class Sems:
    def __init__(self):
        self.count = 0

    def take(self, n):
        at = self.count
        self.count += n
        return at


def layout():
    s = Sems()
    base = {}
    for name, n in (
        ("load", 3),
        ("t_yh", 1), ("t_r", 4), ("t_l", 4), ("t_s", 8),
        ("s_yh", 1), ("s_r", 4), ("s_l", 4), ("s_s", 8),
        ("s0", 8), ("part", 40), ("sq", 8),
        ("st_c", 2), ("st_y", 4), ("st_x", 4), ("st_z", 8),
        ("ga_c", 2), ("ga_y", 4), ("ga_x", 4), ("ga_z", 8),
        ("core", 4), ("rs1", 16), ("rs2", 16), ("rs3", 8),
    ):
        base[name] = s.take(n)
    return base, s.count


BASE, N_SEMS = layout()


def kernel(
    th_ref, tg_ref, thead_hbm, sh_ref, sg_ref, sg8_ref, shead_hbm, ids_ref,
    loss_ref, ghead_hbm, ghid_ref, ggain_ref,
    head, w, h5, scaled, part, got, ssq, sqs, sqr,
    s0, s16, f5, t4, slog, stc, cols,
    st_c, st_y, st_x, st_z, ga_c, ga_y, ga_x, ga_z,
    g_s, gp, gh, own, cs, cr, rs, r1, s2, r2, z3, r3,
    ssem, rsem,
):
    tp = lax.axis_index("tp")
    dp = lax.axis_index("dp")
    c = tp % 2
    z = (tp // 2) % 8
    yh = tp // 16
    x = dp // 2
    yl = dp % 2
    y = yh * 2 + yl

    def dev(xx, yy, zz, cc):
        return ((yy // 2) * 16 + zz * 2 + cc, xx * 2 + yy % 2)

    def zmod(v):
        return (v + 16) % 8

    def peer(axis, j):
        if axis == "c":
            return dev(x, y, z, (c + j) % 2)
        if axis == "x":
            return dev((x + j) % 4, y, z, c)
        if axis == "y":
            return dev(x, (y + j) % 4, z, c)
        return dev(x, y, (z + j) % 8, c)

    size = {"c": 2, "x": 4, "y": 4, "z": 8}
    mine = {"c": c, "x": x, "y": y, "z": z}

    def rc(src, dst, name, i, device):
        at = BASE[name] + i
        return pltpu.make_async_remote_copy(
            src_ref=src, dst_ref=dst, send_sem=ssem.at[at], recv_sem=rsem.at[at],
            device_id=device, device_id_type=MESH,
        )

    def arrived(dst, name, i):
        rc(dst, dst, name, i, peer("c", 1)).wait_recv()

    load_head = pltpu.make_async_copy(thead_hbm, head, ssem.at[BASE["load"]])
    load_w = pltpu.make_async_copy(shead_hbm, w, ssem.at[BASE["load"] + 1])
    load_head.start()
    load_w.start()

    barrier = pltpu.get_barrier_semaphore()
    partners = [peer("c", 1)]
    partners += [peer("x", j) for j in range(1, 4)]
    partners += [peer("y", j) for j in range(1, 4)]
    partners += [dev((x + j) % 4, yh * 2 + 1 - yl, z, c) for j in range(1, 4)]
    partners += [peer("z", j) for j in range(1, 8)]
    for device in partners:
        pl.semaphore_signal(barrier, inc=1, device_id=device, device_id_type=MESH)

    h5[yh, z, c] = th_ref[...]
    s0[dp] = sh_ref[...]
    pl.semaphore_wait(barrier, len(partners))

    yh_peer = dev(x, (y + 2) % 4, z, c)
    sibling = peer("c", 1)
    right = peer("z", 1)
    left = peer("z", 7)

    def yh_copy(buf, name):
        own_block = buf.at[yh, z, c]
        return rc(own_block, own_block, name + "_yh", 0, yh_peer)

    def ring_copies(buf, name, s):
        if s < 3:
            r, l = buf.at[:, zmod(z - s), c], buf.at[:, zmod(z + s), c]
        else:
            r, l = buf.at[0, zmod(z - s), c], buf.at[1, zmod(z + s), c]
        return rc(r, r, name + "_r", s, right), rc(l, l, name + "_l", s, left)

    def ring_arrived(buf, name, s):
        if s < 3:
            r, l = buf.at[:, zmod(z - 1 - s), c], buf.at[:, zmod(z + 1 + s), c]
        else:
            r, l = buf.at[0, zmod(z + 4), c], buf.at[1, zmod(z + 4), c]
        arrived(r, name + "_r", s)
        arrived(l, name + "_l", s)

    def units(s):
        if s == 0:
            return [(0, z)]
        if s == 4:
            return [(7, zmod(z + 4))]
        return [(2 * s - 1, zmod(z - s)), (2 * s, zmod(z + s))]

    def sib_copies(buf, name, s):
        return [
            rc(buf.at[:, zz, c], buf.at[:, zz, c], name + "_s", k, sibling) for k, zz in units(s)
        ]

    def sib_arrived(buf, name, s):
        for k, zz in units(s):
            arrived(buf.at[:, zz, 1 - c], name + "_s", k)

    yh_copy(h5, "t").start()

    def s0_copy(j):
        return rc(s0.at[dp], s0.at[dp], "s0", j, (tp, (dp + j) % 8))

    for j in range(1, 8):
        s0_copy(j).start()

    arrived(h5.at[1 - yh, z, c], "t_yh", 0)
    for cp in ring_copies(h5, "t", 0):
        cp.start()
    for cp in sib_copies(h5, "t", 0):
        cp.start()

    for j in range(1, 8):
        arrived(s0.at[(dp + 8 - j) % 8], "s0", j)
    for d in range(8):
        s16[2 * d : 2 * d + 2, :] = s0[d]
    wide = s16[...]
    inv16 = lax.rsqrt(jnp.sum(wide * wide, -1, keepdims=True) / D_S + epsilon)
    f5[yh, z, c] = (wide * inv16 * sg_ref[...]).astype(bf16)
    yh_copy(f5, "s").start()

    tg = tg_ref[...]

    def part_copy(j, k):
        rows = pl.ds(CHUNK_AT[k], CHUNK_ROWS[k])
        return rc(
            part.at[j, rows], got.at[j - 1, rows], "part", j * 5 + k, (tp, (dp + j) % 8)
        )

    def teacher_chunk(k):
        for i, (_, zz) in enumerate(units(k)):
            for half in range(2):
                block = h5[half, zz].reshape(32, 2048).astype(f32)
                squares = block * block
                total = squares[:, 0:128]
                for lane in range(128, 2048, 128):
                    total = total + squares[:, lane : lane + 128]
                ssq[half, zz] = total
                at = 64 * i + 32 * half
                scaled[at : at + 32, :] = (block * tg).astype(bf16)
        m = CHUNK_ROWS[k]

        def product(j):
            d = (dp + j) % 8
            columns = pl.ds(pl.multiple_of(d * SLICE, SLICE), SLICE)
            part[j, CHUNK_AT[k] : CHUNK_AT[k] + m, :] = jnp.dot(
                scaled[0:m, :], head[:, columns], preferred_element_type=f32
            )

        def send(j, carry):
            product(j)
            part_copy(j, k).start()
            return carry

        lax.fori_loop(1, 8, send, 0)
        product(0)

    load_head.wait()
    for s in range(4):
        ring_arrived(h5, "t", s)
        if s < 3:
            for cp in ring_copies(h5, "t", s + 1):
                cp.start()
        for cp in sib_copies(h5, "t", s + 1):
            cp.start()
        if s == 2:
            arrived(f5.at[1 - yh, z, c], "s_yh", 0)
            for cp in ring_copies(f5, "s", 0):
                cp.start()
            for cp in sib_copies(f5, "s", 0):
                cp.start()
        sib_arrived(h5, "t", s)
        teacher_chunk(s)
    sib_arrived(h5, "t", 4)
    teacher_chunk(4)

    sums = jnp.sum(ssq[...].reshape(TOKENS, 128).T, 0, keepdims=True)
    sqs[...] = jnp.broadcast_to(sums, (8, TOKENS))

    def sq_copy(j):
        return rc(sqs, sqr.at[j - 1], "sq", j, (tp, (dp + j) % 8))

    for j in range(1, 8):
        sq_copy(j).start()

    for s in range(4):
        ring_arrived(f5, "s", s)
        if s < 3:
            for cp in ring_copies(f5, "s", s + 1):
                cp.start()
        for cp in sib_copies(f5, "s", s + 1):
            cp.start()
    for s in range(5):
        sib_arrived(f5, "s", s)

    load_w.wait()
    for half in range(2):
        for quarter in range(2):
            rows = f5[half, 4 * quarter : 4 * quarter + 4].reshape(128, D_S)
            at = half * 256 + quarter * 128
            slog[at : at + 128, :] = jnp.dot(rows, w[...], preferred_element_type=f32)
    ids = jnp.broadcast_to(ids_ref[...], (128, TOKENS)).T
    ids = jnp.concatenate([ids, ids], axis=1)
    first = (tp * 8 + dp) * SLICE
    target_mask = ids == first + lax.broadcasted_iota(jnp.int32, (TOKENS, SLICE), 1)
    student = slog[...]
    s_top = jnp.max(student, -1, keepdims=True)
    s_total = jnp.sum(jnp.exp(student - s_top), -1, keepdims=True)
    target = jnp.sum(jnp.where(target_mask, student, 0.0), -1, keepdims=True)
    lane = lax.broadcasted_iota(jnp.int32, (TOKENS, 128), 1)
    stc[...] = jnp.where(
        lane == 3, s_top, jnp.where(lane == 4, s_total, jnp.where(lane == 5, target, 0.0))
    )

    for j in range(1, 8):
        arrived(sqr.at[j - 1], "sq", j)
    square_total = sqs[...]
    for j in range(7):
        square_total = square_total + sqr[j]
    t_inv = lax.rsqrt(square_total / D_T + epsilon)
    t_inv = jnp.broadcast_to(t_inv[0:1, :], (128, TOKENS)).T
    t_inv = jnp.concatenate([t_inv, t_inv], axis=1)
    for k in range(5):
        for j in range(1, 8):
            rows = pl.ds(CHUNK_AT[k], CHUNK_ROWS[k])
            arrived(got.at[j - 1, rows], "part", j * 5 + k)
        for i, (_, zz) in enumerate(units(k)):
            at = CHUNK_AT[k] + 64 * i
            total = part[0, at : at + 64, :]
            for j in range(7):
                total = total + got[j, at : at + 64, :]
            t4[0, zz] = total[0:32]
            t4[1, zz] = total[32:64]
    teacher = t4[...].reshape(TOKENS, SLICE) * t_inv

    t_top = jnp.max(teacher, -1, keepdims=True)
    t_exp = jnp.exp(teacher - t_top)
    t_total = jnp.sum(t_exp, -1, keepdims=True)
    cross = jnp.sum(t_exp * (teacher - student), -1, keepdims=True)
    packed = jnp.where(
        lane == 0, t_top, jnp.where(lane == 1, t_total, jnp.where(lane == 2, cross, stc[...]))
    )
    stats = packed.T[0:8, :]

    def exchange(buf, name, axis, value):
        buf[mine[axis]] = value
        for j in range(1, size[axis]):
            exchange_copy(buf, name, axis, j).start()

    def exchange_copy(buf, name, axis, j):
        slot = buf.at[mine[axis]]
        return rc(slot, slot, name + "_" + axis, j, peer(axis, j))

    def exchanged(buf, name, axis):
        n = size[axis]
        for j in range(1, n):
            arrived(buf.at[(mine[axis] + n - j) % n], name + "_" + axis, j)
        return [buf[i] for i in range(n)]

    def merged(parts):
        t_m = functools.reduce(jnp.maximum, [p[0:1] for p in parts])
        s_m = functools.reduce(jnp.maximum, [p[3:4] for p in parts])
        t_s = c_s = s_s = tgt = 0.0
        for p in parts:
            t_f = jnp.exp(p[0:1] - t_m)
            s_f = jnp.exp(p[3:4] - s_m)
            t_s = t_s + p[1:2] * t_f
            c_s = c_s + p[2:3] * t_f
            s_s = s_s + p[4:5] * s_f
            tgt = tgt + p[5:6]
        row = lax.broadcasted_iota(jnp.int32, (8, TOKENS), 0)
        out = jnp.zeros((8, TOKENS), f32)
        for i, v in enumerate((t_m, t_s, c_s, s_m, s_s, tgt)):
            out = jnp.where(row == i, v, out)
        return out

    for axis, buf in (("c", st_c), ("y", st_y), ("x", st_x), ("z", st_z)):
        exchange(buf, "st", axis, stats)
        stats = merged(exchanged(buf, "st", axis))

    t_lse = stats[0:1] + jnp.log(stats[1:2])
    s_lse = stats[3:4] + jnp.log(stats[4:5])
    loss_ref[...] = (
        stats[2:3] / stats[1:2] - t_lse + s_lse + hard_weight * (s_lse - stats[5:6])
    )
    t_col = jnp.broadcast_to(t_lse, (128, TOKENS)).T
    s_col = jnp.broadcast_to(s_lse, (128, TOKENS)).T
    t_prob = jnp.exp(teacher - jnp.concatenate([t_col, t_col], axis=1))
    s_prob = jnp.exp(student - jnp.concatenate([s_col, s_col], axis=1))
    onehot = target_mask.astype(f32)
    g = (loss_scale * (s_prob - t_prob + hard_weight * (s_prob - onehot))).astype(bf16)
    g_s[...] = g

    p = lax.broadcasted_iota(jnp.int32, (TOKENS, TOKENS), 0)
    q = lax.broadcasted_iota(jnp.int32, (TOKENS, TOKENS), 1)
    source = (
        ((p >> 5) & 1) * 256
        + ((p >> 1) & 7) * 32
        + (p >> 8) * 16
        + ((p >> 6) & 3) * 4
        + ((p >> 4) & 1) * 2
        + (p & 1)
    )
    perm = jnp.where(q == source, 1.0, 0.0).astype(bf16)
    gp[...] = jnp.dot(perm, g, preferred_element_type=f32).astype(bf16)

    def core_copy(ch):
        return rc(cs.at[ch], cr.at[ch], "core", ch, sibling)

    other_rows = pl.ds(pl.multiple_of((1 - c) * 256, 256), 256)
    own_rows = pl.ds(pl.multiple_of(c * 256, 256), 256)
    for ch in ORDER:
        for tile in range(2):
            at = ch * WIDE + tile * 512
            cs[ch, :, tile * 512 : tile * 512 + 512] = lax.dot_general(
                gp[other_rows, :], w[at : at + 512, :], NT, preferred_element_type=f32
            ).astype(bf16)
        core_copy(ch).start()
    for ch in ORDER:
        for tile in range(2):
            at = ch * WIDE + tile * 512
            own[ch, :, tile * 512 : tile * 512 + 512] = lax.dot_general(
                gp[own_rows, :], w[at : at + 512, :], NT, preferred_element_type=f32
            )

    def rs1_copy(ch, j):
        if ch < 2:
            return rc(rs.at[ch, (x + j) % 4], r1.at[ch, j - 1], "rs1", ch * 4 + j, peer("x", j))
        return rc(rs.at[ch, :, (y + j) % 4], r1.at[ch, j - 1], "rs1", ch * 4 + j, peer("y", j))

    for ch in ORDER:
        arrived(cr.at[ch], "core", ch)
        both = own[ch] + cr[ch].astype(f32)
        rs[ch] = both.astype(bf16).reshape(4, 4, 16, WIDE)
        for j in range(1, 4):
            rs1_copy(ch, j).start()

    ones = jnp.ones((8, SLICE), bf16)

    def head_tile(i, carry):
        at = pl.ds(pl.multiple_of(i * 512, 512), 512)
        features = f5[:, :, :, :, at].reshape(TOKENS, 512)
        tile = jnp.dot(features.T, g_s[...], preferred_element_type=f32)
        gh[at, :] = tile.astype(bf16)
        product = tile * w[at, :].astype(f32)
        high = product.astype(bf16)
        low = (product - high.astype(f32)).astype(bf16)
        row = lax.dot_general(ones, high, NT, preferred_element_type=f32) + lax.dot_general(
            ones, low, NT, preferred_element_type=f32
        )
        cols[...] = jnp.where(
            lax.broadcasted_iota(jnp.int32, (8, 512), 0) == i, row, cols[...]
        )
        return carry

    cols[...] = jnp.zeros((8, 512), f32)
    lax.fori_loop(0, 8, head_tile, 0)
    store_head = pltpu.make_async_copy(gh, ghead_hbm, ssem.at[BASE["load"] + 2])
    store_head.start()
    gain = cols[...]
    for axis, buf in (("c", ga_c), ("x", ga_x)):
        exchange(buf, "ga", axis, gain)
        gain = functools.reduce(jnp.add, exchanged(buf, "ga", axis))
    exchange(ga_y, "ga", "y", gain)

    def rs2_copy(ch, j):
        if ch < 2:
            return rc(s2.at[ch, (y + j) % 4], r2.at[ch, j - 1], "rs2", ch * 4 + j, peer("y", j))
        return rc(s2.at[ch, (x + j) % 4], r2.at[ch, j - 1], "rs2", ch * 4 + j, peer("x", j))

    for ch in ORDER:
        for j in range(1, 4):
            arrived(r1.at[ch, j - 1], "rs1", ch * 4 + j)
        kept = rs[ch, x] if ch < 2 else rs[ch, :, y]
        total = kept.astype(f32)
        for j in range(3):
            total = total + r1[ch, j].astype(f32)
        s2[ch] = total.astype(bf16)
        for j in range(1, 4):
            rs2_copy(ch, j).start()

    gain = functools.reduce(jnp.add, exchanged(ga_y, "ga", "y"))
    exchange(ga_z, "ga", "z", gain)

    for ch in ORDER:
        for j in range(1, 4):
            arrived(r2.at[ch, j - 1], "rs2", ch * 4 + j)
        kept = s2[ch, y] if ch < 2 else s2[ch, x]
        total = kept.astype(f32)
        for j in range(3):
            total = total + r2[ch, j].astype(f32)
        for zz in range(8):
            z3[zz, :, ch * WIDE : ch * WIDE + WIDE] = total[2 * zz : 2 * zz + 2, :]

    def rs3_copy(j):
        return rc(z3.at[(z + j) % 8], r3.at[j - 1], "rs3", j, peer("z", j))

    for j in range(1, 8):
        rs3_copy(j).start()

    own_wide = sh_ref[...]
    own_inv = lax.rsqrt(jnp.sum(own_wide * own_wide, -1, keepdims=True) / D_S + epsilon)
    own_normed = own_wide * own_inv
    gain = functools.reduce(jnp.add, exchanged(ga_z, "ga", "z"))
    ggain_ref[...] = gain / sg8_ref[...]

    for j in range(1, 8):
        arrived(r3.at[j - 1], "rs3", j)
    grad_features = z3[z]
    for j in range(7):
        grad_features = grad_features + r3[j]
    grad_normed = grad_features * sg_ref[...]
    inner = jnp.sum(grad_normed * own_normed, -1, keepdims=True) / D_S
    ghid_ref[...] = own_inv * (grad_normed - own_normed * inner)

    for buf, name in ((h5, "t"), (f5, "s")):
        yh_copy(buf, name).wait_send()
        for s in range(4):
            for cp in ring_copies(buf, name, s):
                cp.wait_send()
        for s in range(5):
            for cp in sib_copies(buf, name, s):
                cp.wait_send()
    for j in range(1, 8):
        s0_copy(j).wait_send()
        sq_copy(j).wait_send()
        rs3_copy(j).wait_send()
        for k in range(5):
            part_copy(j, k).wait_send()
    for name, bufs in (("st", (st_c, st_y, st_x, st_z)), ("ga", (ga_c, ga_y, ga_x, ga_z))):
        for axis, buf in zip("cyxz", bufs):
            for j in range(1, size[axis]):
                exchange_copy(buf, name, axis, j).wait_send()
    for ch in range(4):
        core_copy(ch).wait_send()
        for j in range(1, 4):
            rs1_copy(ch, j).wait_send()
            rs2_copy(ch, j).wait_send()
    store_head.wait()


def shards(
    teacher_hidden,
    teacher_gain,
    teacher_head,
    student_hidden,
    student_gain,
    student_head,
    token_ids,
):
    vmem = pl.BlockSpec(memory_space=pltpu.VMEM)
    hbm = pl.BlockSpec(memory_space=pl.ANY)
    gain_wide = student_gain.astype(f32)
    row8 = (8, TOKENS)
    scratch = [
        ((2048, 2048), bf16), ((D_S, SLICE), bf16), ((2, 8, 2, 16, 2048), bf16),
        ((128, 2048), bf16), ((8, TOKENS, SLICE), f32), ((7, TOKENS, SLICE), f32),
        ((2, 8, 32, 128), f32), (row8, f32), ((7,) + row8, f32),
        ((8, 2, D_S), f32), ((16, D_S), f32), ((2, 8, 2, 16, D_S), bf16),
        ((2, 8, 32, SLICE), f32), ((TOKENS, SLICE), f32), ((TOKENS, 128), f32), ((8, 512), f32),
        ((2,) + row8, f32), ((4,) + row8, f32), ((4,) + row8, f32), ((8,) + row8, f32),
        ((2,) + row8, f32), ((4,) + row8, f32), ((4,) + row8, f32), ((8,) + row8, f32),
        ((TOKENS, SLICE), bf16), ((TOKENS, SLICE), bf16), ((D_S, SLICE), bf16),
        ((4, 256, WIDE), f32), ((4, 256, WIDE), bf16), ((4, 256, WIDE), bf16),
        ((4, 4, 4, 16, WIDE), bf16), ((4, 3, 4, 16, WIDE), bf16),
        ((4, 4, 16, WIDE), bf16), ((4, 3, 16, WIDE), bf16),
        ((8, 2, D_S), f32), ((7, 2, D_S), f32),
    ]
    loss, grad_head, grad_hidden, grad_gain = pl.pallas_call(
        kernel,
        out_shape=(
            jax.ShapeDtypeStruct((1, TOKENS), f32),
            jax.ShapeDtypeStruct((D_S, SLICE), bf16),
            jax.ShapeDtypeStruct((2, D_S), f32),
            jax.ShapeDtypeStruct((8, 512), f32),
        ),
        in_specs=[vmem, vmem, hbm, vmem, vmem, vmem, hbm, vmem],
        out_specs=(vmem, hbm, vmem, vmem),
        scratch_shapes=[pltpu.VMEM(shape, dtype) for shape, dtype in scratch]
        + [pltpu.SemaphoreType.DMA((N_SEMS,)), pltpu.SemaphoreType.DMA((N_SEMS,))],
        compiler_params=pltpu.CompilerParams(
            collective_id=0, has_side_effects=True, vmem_limit_bytes=56 * 1024 * 1024
        ),
        cost_estimate=pl.CostEstimate(
            flops=7_600_000_000, bytes_accessed=13_000_000, transcendentals=600_000
        ),
    )(
        teacher_hidden,
        teacher_gain.astype(f32).reshape(1, 2048),
        teacher_head,
        student_hidden.astype(f32),
        gain_wide.reshape(1, D_S),
        gain_wide.reshape(8, 512),
        student_head,
        token_ids.reshape(1, TOKENS),
    )
    return (
        loss.reshape(TOKENS),
        grad_hidden.astype(bf16),
        grad_gain.reshape(D_S),
        grad_head,
    )


def solution(mesh):
    in_specs = (
        P("tp", "dp"),
        P("dp"),
        P("dp", "tp"),
        P(("tp", "dp"), None),
        P(),
        P(None, ("tp", "dp")),
        P(),
    )
    out_specs = (P(), P(("tp", "dp"), None), P(), P(None, ("tp", "dp")))
    return jax.shard_map(shards, mesh=mesh, in_specs=in_specs, out_specs=out_specs, check_vma=False)
```

time: 1420 us -> 135 us (0.10)
  waiting for transfers between devices: 1110 us -> 0 us
  blocking collectives: 243 us -> 0 us
  Pallas kernels: 0 us -> 121 us
  matrix products: 24.3 us -> 0 us
    all_gather x2 -> x0, waiting for transfers between devices: 763 us -> none  [the longest x1 677 us: shards(): full_rows = lax.all_gather(student_hidden, ('tp', 'dp'), axis=0, tiled=True)]
    unnamed x5 -> x0, waiting for transfers between devices: 267 us -> none
    psum x3 -> x0, blocking collectives: 166 us -> none  [the longest x2 151 us: shards(): lax.psum((jnp.sum(teacher_exp, -1), jnp.sum(student_exp, -1), jnp.sum(tea...]
    pallas_call x0 -> x1, Pallas kernels: none -> 121 us  [shards(): pl.pallas_call(kernel, out_shape=(jax.ShapeDtypeStruct((1, TOKENS), f32),...]
    reduce_scatter x1 -> x0, waiting for transfers between devices: 79.3 us -> none  [shards(): lax.psum_scatter(partial_logits, 'dp', scatter_dimension=1, tiled=True)]
    pmax x1 -> x0, blocking collectives: 77.2 us -> none  [shards(): lax.pmax((jnp.max(teacher_logits, -1), jnp.max(student_logits, -1)), ('tp...]
    dot_general x4 -> x0, matrix products: 24.3 us -> none  [the longest x1 10.5 us: shards(): jnp.dot(teacher_scaled, teacher_head, preferred_element_type=jnp.float32)]
  transfers between devices with their start and end apart: 4 -> 0, of which waited for: 4 -> 0; matrix products, arithmetic and copies ran while one was open for 2% -> 0% of each run, Pallas kernels for 0% -> 0%
where the time goes in v1:
time: 135 us; the launch traced here: 134 us
  Pallas kernels  121 us (90%)
  local copies, waits for them, and re-layouts  6.92 us (5%)
  other arithmetic  5.31 us (4%)
    pallas_call x1, Pallas kernels, shards(): pl.pallas_call(kernel, out_shape=(jax.ShapeDtypeStruct((1, TOKENS), f32),...  121 us
    unnamed x3, local copies, waits for them, and re-layouts  5.61 us

profile of v1, /device:TPU:1, one launch (start us, length us, event | category | flops | bytes accessed | tf_op | source)
XLA Modules:
  0.0 134.3 jit_solution(12003790110619981869)
XLA Ops:
  0.6 1.3 reshape.35
  1.9 1.3 reshape.31.sg8_ref
  3.2 1.3 convert_element_type.11
  4.5 1.3 convert_element_type.10.sh_ref
  5.9 121.5 %shard_map.102 = (f32[1,512]{1,0:T(1,128)}, bf16[4096,256]{1,0:T(8,128)(2,1)}, f32[2,4096]{1,0:T(2,128)}, f32[8,512]{1,0:T(8,128)}) custom-call(bf16[16,2048]{1,0:T(8,128)(2,1)} %th_ref.1, f32[1,2048]{1,0:T(1,128)} %bitcast.9, bf16[2048,2048]{1,0:T(8,128)(2,1)} %thead_hbm.1, f32[2,4096]{1,0:T(2,128)} %convert_element_type.10.sh_ref, f32[1,4096]{1,0:T(1,128)} %bitcast.6, ...), custom_call_target="tpu_custom_call" | custom-call | flops 7600000000 | bytes 13000000 | tf_op jit(solution)/shard_map/pallas_call | solution.py:533
  127.4 1.4 %convert_element_type.12 = bf16[2,4096]{1,0:T(2,128)(2,1)} convert(f32[2,4096]{1,0:T(2,128)} %get-tuple-element.9) | non-fusion elementwise | flops 8192 | bytes 49152 | tf_op jit(solution)/shard_map/convert_element_type | solution.py:563
  128.7 1.3 copy.11
  130.1 1.2 copy.14
  131.3 3.0 %copy.15 = bf16[4096,256]{1,0:T(8,128)(2,1)} copy(bf16[4096,256]{1,0:T(8,128)(2,1)} %get-tuple-element.19) | data formatting | bytes 4194304

commit v2 on v1

--- a/solution.py
+++ b/solution.py
@@ -21,8 +21,8 @@
 bf16 = jnp.bfloat16
 NT = (((1,), (1,)), ((), ()))
 
-CHUNK_ROWS = (64, 128, 128, 128, 64)
-CHUNK_AT = (0, 64, 192, 320, 448)
+CHUNK_ROWS = (32, 64, 64, 64, 32)
+CHUNK_AT = (0, 32, 96, 160, 224)
 ORDER = (0, 2, 1, 3)
 WIDE = 1024
 
@@ -43,11 +43,11 @@
     for name, n in (
         ("load", 3),
         ("t_yh", 1), ("t_r", 4), ("t_l", 4), ("t_s", 8),
-        ("s_yh", 1), ("s_r", 4), ("s_l", 4), ("s_s", 8),
-        ("s0", 8), ("part", 40), ("sq", 8),
-        ("st_c", 2), ("st_y", 4), ("st_x", 4), ("st_z", 8),
-        ("ga_c", 2), ("ga_y", 4), ("ga_x", 4), ("ga_z", 8),
-        ("core", 4), ("rs1", 16), ("rs2", 16), ("rs3", 8),
+        ("s_yh", 1), ("s_r", 8), ("s_l", 8), ("s_s", 8),
+        ("s0", 8), ("ex", 50), ("sq", 8),
+        ("st_cx", 8), ("st_y", 4), ("st_z", 8),
+        ("ga_cx", 8), ("ga_y", 4), ("ga_z", 8),
+        ("core", 4), ("q1", 8), ("q2", 8), ("rs2", 16), ("rs3", 8),
     ):
         base[name] = s.take(n)
     return base, s.count
@@ -57,12 +57,12 @@
 
 
 def kernel(
-    th_ref, tg_ref, thead_hbm, sh_ref, sg_ref, sg8_ref, shead_hbm, ids_ref,
+    th_ref, tg_ref, thead_hbm, sh_ref, sg_ref, shead_hbm, ids_ref,
     loss_ref, ghead_hbm, ghid_ref, ggain_ref,
-    head, w, h5, scaled, part, got, ssq, sqs, sqr,
+    head, w, wt, h5, scaled, pa, pb, ya, xa1, xa2, xb1, xb2, yb, ssq, sqs, sqr,
     s0, s16, f5, t4, slog, stc, cols,
-    st_c, st_y, st_x, st_z, ga_c, ga_y, ga_x, ga_z,
-    g_s, gp, gh, own, cs, cr, rs, r1, s2, r2, z3, r3,
+    st_cx, st_y, st_z, ga_cx, ga_y, ga_z,
+    g_s, gp, perm, gh, own, cs, cr, rs, q1, q2, s2, r2, zf, zb, r3, unfolded,
     ssem, rsem,
 ):
     tp = lax.axis_index("tp")
@@ -87,10 +87,13 @@
             return dev((x + j) % 4, y, z, c)
         if axis == "y":
             return dev(x, (y + j) % 4, z, c)
+        if axis == "cx":
+            at = (x * 2 + c + j) % 8
+            return dev(at // 2, y, z, at % 2)
         return dev(x, y, (z + j) % 8, c)
 
-    size = {"c": 2, "x": 4, "y": 4, "z": 8}
-    mine = {"c": c, "x": x, "y": y, "z": z}
+    size = {"cx": 8, "y": 4, "z": 8}
+    mine = {"cx": x * 2 + c, "y": y, "z": z}
 
     def rc(src, dst, name, i, device):
         at = BASE[name] + i
@@ -109,7 +112,7 @@
 
     barrier = pltpu.get_barrier_semaphore()
     partners = [peer("c", 1)]
-    partners += [peer("x", j) for j in range(1, 4)]
+    partners += [dev((x + j) % 4, y, z, cc) for j in range(1, 4) for cc in range(2)]
     partners += [peer("y", j) for j in range(1, 4)]
     partners += [dev((x + j) % 4, yh * 2 + 1 - yl, z, c) for j in range(1, 4)]
     partners += [peer("z", j) for j in range(1, 8)]
@@ -117,7 +120,7 @@
         pl.semaphore_signal(barrier, inc=1, device_id=device, device_id_type=MESH)
 
     h5[yh, z, c] = th_ref[...]
-    s0[dp] = sh_ref[...]
+    s0[dp] = sh_ref[...].astype(f32)
     pl.semaphore_wait(barrier, len(partners))
 
     yh_peer = dev(x, (y + 2) % 4, z, c)
@@ -125,9 +128,11 @@
     right = peer("z", 1)
     left = peer("z", 7)
 
+    y_outer = dev(x, 3 - y, z, c)
+
     def yh_copy(buf, name):
         own_block = buf.at[yh, z, c]
-        return rc(own_block, own_block, name + "_yh", 0, yh_peer)
+        return rc(own_block, own_block, name + "_yh", 0, yh_peer if name == "t" else y_outer)
 
     def ring_copies(buf, name, s):
         if s < 3:
@@ -144,6 +149,30 @@
         arrived(r, name + "_r", s)
         arrived(l, name + "_l", s)
 
+    def half_copies(s, half):
+        r, l = f5.at[half, zmod(z - s), c], f5.at[half, zmod(z + s), c]
+        copies = []
+        if s < 3 or half == 0:
+            copies.append(rc(r, r, "s_r", 2 * s + half, right))
+        if s < 3 or half == 1:
+            copies.append(rc(l, l, "s_l", 2 * s + half, left))
+        return copies
+
+    def half_arrived(s, half):
+        if s < 3 or half == 0:
+            arrived(f5.at[half, zmod(z - 1 - s), c], "s_r", 2 * s + half)
+        if s < 3 or half == 1:
+            arrived(f5.at[half, zmod(z + 1 + s), c], "s_l", 2 * s + half)
+
+    def student_step(s, half):
+        half_arrived(s, half)
+        if s < 3:
+            for cp in half_copies(s + 1, half):
+                cp.start()
+        if half == 1:
+            for cp in sib_copies(f5, "s", s + 1):
+                cp.start()
+
     def units(s):
         if s == 0:
             return [(0, z)]
@@ -180,16 +209,60 @@
         s16[2 * d : 2 * d + 2, :] = s0[d]
     wide = s16[...]
     inv16 = lax.rsqrt(jnp.sum(wide * wide, -1, keepdims=True) / D_S + epsilon)
-    f5[yh, z, c] = (wide * inv16 * sg_ref[...]).astype(bf16)
+    gain_row = sg_ref[...].astype(f32).reshape(1, D_S)
+    f5[yh, z, c] = (wide * inv16 * gain_row).astype(bf16)
     yh_copy(f5, "s").start()
 
-    tg = tg_ref[...]
-
-    def part_copy(j, k):
-        rows = pl.ds(CHUNK_AT[k], CHUNK_ROWS[k])
-        return rc(
-            part.at[j, rows], got.at[j - 1, rows], "part", j * 5 + k, (tp, (dp + j) % 8)
+    tg = tg_ref[...].astype(f32).reshape(1, 2048)
+
+    x_right = peer("x", 1)
+    x_left = peer("x", 3)
+    y_pair = dev(x, yh * 2 + 1 - yl, z, c)
+
+    def span(k, part):
+        at, n = CHUNK_AT[k], CHUNK_ROWS[k]
+        return {"all": pl.ds(at, n), "r": pl.ds(at, n // 2), "l": pl.ds(at + n // 2, n // 2)}[part]
+
+    def ex_copies(k, step):
+        every, rows_r, rows_l = span(k, "all"), span(k, "r"), span(k, "l")
+        a_y = (pa.at[:, 1, every], ya.at[:, every], 0, y_pair)
+        a_x1r = (pa.at[2, 0, rows_r], xa1.at[0, rows_r], 1, x_right)
+        a_x1l = (pa.at[2, 0, rows_l], xa1.at[1, rows_l], 2, x_left)
+        a_x2r = (pa.at[1, 0, every], xa2.at[0, every], 3, x_right)
+        a_x2l = (pa.at[3, 0, every], xa2.at[1, every], 4, x_left)
+        b_x1r = (pb.at[2, :, rows_r], xb1.at[0, :, rows_r], 5, x_right)
+        b_x1l = (pb.at[2, :, rows_l], xb1.at[1, :, rows_l], 6, x_left)
+        b_x2r = (pb.at[1, :, every], xb2.at[0, :, every], 7, x_right)
+        b_x2l = (pb.at[3, :, every], xb2.at[1, :, every], 8, x_left)
+        b_y = (pb.at[0, 1, every], yb.at[every], 9, y_pair)
+        steps = (
+            (a_y, b_x1r, b_x1l), (a_x1r, a_x1l, b_x2r, b_x2l), (a_x2r, a_x2l, b_y),
         )
+        return [rc(src, dst, "ex", k * 10 + i, device) for src, dst, i, device in steps[step]]
+
+    def ex_arrived(k, step):
+        for cp in ex_copies(k, step):
+            cp.wait_recv()
+
+    def ex_send(k, step):
+        for cp in ex_copies(k, step):
+            cp.start()
+
+    def ex_second(k):
+        every, rows_r, rows_l = span(k, "all"), span(k, "r"), span(k, "l")
+        ex_arrived(k, 0)
+        pb[1, :, rows_r] += xb1[0, :, rows_r]
+        pb[3, :, rows_l] += xb1[1, :, rows_l]
+        pa[:, 0, every] += ya[:, every]
+        ex_send(k, 1)
+
+    def ex_third(k):
+        every, rows_r, rows_l = span(k, "all"), span(k, "r"), span(k, "l")
+        ex_arrived(k, 1)
+        pa[1, 0, rows_r] += xa1[0, rows_r]
+        pa[3, 0, rows_l] += xa1[1, rows_l]
+        pb[0, :, every] += xb2[0, :, every] + xb2[1, :, every]
+        ex_send(k, 2)
 
     def teacher_chunk(k):
         for i, (_, zz) in enumerate(units(k)):
@@ -200,25 +273,30 @@
                 for lane in range(128, 2048, 128):
                     total = total + squares[:, lane : lane + 128]
                 ssq[half, zz] = total
-                at = 64 * i + 32 * half
+                at = CHUNK_ROWS[k] * half + 32 * i
                 scaled[at : at + 32, :] = (block * tg).astype(bf16)
         m = CHUNK_ROWS[k]
 
-        def product(j):
-            d = (dp + j) % 8
+        def product(j, carry):
+            xo, yo = j // 2, j % 2
+            d = ((x + xo) % 4) * 2 + (yl + yo) % 2
             columns = pl.ds(pl.multiple_of(d * SLICE, SLICE), SLICE)
-            part[j, CHUNK_AT[k] : CHUNK_AT[k] + m, :] = jnp.dot(
-                scaled[0:m, :], head[:, columns], preferred_element_type=f32
-            )
-
-        def send(j, carry):
-            product(j)
-            part_copy(j, k).start()
+            both = jnp.dot(scaled[0 : 2 * m, :], head[:, columns], preferred_element_type=f32)
+            pa[xo, yo, CHUNK_AT[k] : CHUNK_AT[k] + m, :] = both[0:m]
+            pb[xo, yo, CHUNK_AT[k] : CHUNK_AT[k] + m, :] = both[m : 2 * m]
             return carry
 
-        lax.fori_loop(1, 8, send, 0)
-        product(0)
-
+        lax.fori_loop(0, 8, product, 0)
+        ex_send(k, 0)
+
+    load_w.wait()
+
+    def turn(i, carry):
+        at = pl.ds(pl.multiple_of(i * 512, 512), 512)
+        wt[:, at] = w[at, :].T
+        return carry
+
+    lax.fori_loop(0, 8, turn, 0)
     load_head.wait()
     for s in range(4):
         ring_arrived(h5, "t", s)
@@ -227,16 +305,25 @@
                 cp.start()
         for cp in sib_copies(h5, "t", s + 1):
             cp.start()
-        if s == 2:
+        if s == 0:
             arrived(f5.at[1 - yh, z, c], "s_yh", 0)
-            for cp in ring_copies(f5, "s", 0):
-                cp.start()
+            for half in range(2):
+                for cp in half_copies(0, half):
+                    cp.start()
             for cp in sib_copies(f5, "s", 0):
                 cp.start()
+        if s >= 2:
+            student_step(0, s - 2)
         sib_arrived(h5, "t", s)
         teacher_chunk(s)
+        if s >= 1:
+            ex_second(s - 1)
+        if s >= 2:
+            ex_third(s - 2)
+    student_step(1, 0)
     sib_arrived(h5, "t", 4)
     teacher_chunk(4)
+    student_step(1, 1)
 
     sums = jnp.sum(ssq[...].reshape(TOKENS, 128).T, 0, keepdims=True)
     sqs[...] = jnp.broadcast_to(sums, (8, TOKENS))
@@ -247,17 +334,30 @@
     for j in range(1, 8):
         sq_copy(j).start()
 
-    for s in range(4):
-        ring_arrived(f5, "s", s)
-        if s < 3:
-            for cp in ring_copies(f5, "s", s + 1):
-                cp.start()
-        for cp in sib_copies(f5, "s", s + 1):
-            cp.start()
+    ex_second(3)
+    ex_third(2)
+    student_step(2, 0)
+    ex_second(4)
+    student_step(2, 1)
+    ex_third(3)
+    student_step(3, 0)
+    ex_third(4)
+    student_step(3, 1)
     for s in range(5):
         sib_arrived(f5, "s", s)
 
-    load_w.wait()
+    p = lax.broadcasted_iota(jnp.int32, (TOKENS, TOKENS), 0)
+    q = lax.broadcasted_iota(jnp.int32, (TOKENS, TOKENS), 1)
+    source = (
+        ((p >> 5) & 1) * 256
+        + ((p >> 1) & 7) * 32
+        + (p >> 8) * 16
+        + ((p >> 6) & 3) * 4
+        + ((p >> 4) & 1) * 2
+        + (p & 1)
+    )
+    perm[...] = jnp.where(q == source, 1.0, 0.0).astype(bf16)
+
     for half in range(2):
         for quarter in range(2):
             rows = f5[half, 4 * quarter : 4 * quarter + 4].reshape(128, D_S)
@@ -285,16 +385,11 @@
     t_inv = jnp.broadcast_to(t_inv[0:1, :], (128, TOKENS)).T
     t_inv = jnp.concatenate([t_inv, t_inv], axis=1)
     for k in range(5):
-        for j in range(1, 8):
-            rows = pl.ds(CHUNK_AT[k], CHUNK_ROWS[k])
-            arrived(got.at[j - 1, rows], "part", j * 5 + k)
+        ex_arrived(k, 2)
         for i, (_, zz) in enumerate(units(k)):
-            at = CHUNK_AT[k] + 64 * i
-            total = part[0, at : at + 64, :]
-            for j in range(7):
-                total = total + got[j, at : at + 64, :]
-            t4[0, zz] = total[0:32]
-            t4[1, zz] = total[32:64]
+            rows = pl.ds(CHUNK_AT[k] + 32 * i, 32)
+            t4[0, zz] = pa[0, 0, rows] + xa2[0, rows] + xa2[1, rows]
+            t4[1, zz] = pb[0, 0, rows] + yb[rows]
     teacher = t4[...].reshape(TOKENS, SLICE) * t_inv
 
     t_top = jnp.max(teacher, -1, keepdims=True)
@@ -338,7 +433,7 @@
             out = jnp.where(row == i, v, out)
         return out
 
-    for axis, buf in (("c", st_c), ("y", st_y), ("x", st_x), ("z", st_z)):
+    for axis, buf in (("cx", st_cx), ("y", st_y), ("z", st_z)):
         exchange(buf, "st", axis, stats)
         stats = merged(exchanged(buf, "st", axis))
 
@@ -355,49 +450,67 @@
     g = (loss_scale * (s_prob - t_prob + hard_weight * (s_prob - onehot))).astype(bf16)
     g_s[...] = g
 
-    p = lax.broadcasted_iota(jnp.int32, (TOKENS, TOKENS), 0)
-    q = lax.broadcasted_iota(jnp.int32, (TOKENS, TOKENS), 1)
-    source = (
-        ((p >> 5) & 1) * 256
-        + ((p >> 1) & 7) * 32
-        + (p >> 8) * 16
-        + ((p >> 6) & 3) * 4
-        + ((p >> 4) & 1) * 2
-        + (p & 1)
-    )
-    perm = jnp.where(q == source, 1.0, 0.0).astype(bf16)
-    gp[...] = jnp.dot(perm, g, preferred_element_type=f32).astype(bf16)
+    gp[...] = jnp.dot(perm[...], g, preferred_element_type=f32).astype(bf16)
 
     def core_copy(ch):
         return rc(cs.at[ch], cr.at[ch], "core", ch, sibling)
 
     other_rows = pl.ds(pl.multiple_of((1 - c) * 256, 256), 256)
     own_rows = pl.ds(pl.multiple_of(c * 256, 256), 256)
-    for ch in ORDER:
+    def product_of(rows, ch, tile):
+        at = ch * WIDE + tile * 512
+        return jnp.dot(gp[rows, :], wt[:, at : at + 512], preferred_element_type=f32)
+
+    def other_part(ch):
         for tile in range(2):
-            at = ch * WIDE + tile * 512
-            cs[ch, :, tile * 512 : tile * 512 + 512] = lax.dot_general(
-                gp[other_rows, :], w[at : at + 512, :], NT, preferred_element_type=f32
-            ).astype(bf16)
+            cs[ch, :, tile * 512 : tile * 512 + 512] = product_of(other_rows, ch, tile).astype(bf16)
         core_copy(ch).start()
-    for ch in ORDER:
+
+    def own_part(ch):
         for tile in range(2):
-            at = ch * WIDE + tile * 512
-            own[ch, :, tile * 512 : tile * 512 + 512] = lax.dot_general(
-                gp[own_rows, :], w[at : at + 512, :], NT, preferred_element_type=f32
-            )
-
-    def rs1_copy(ch, j):
+            own[ch, :, tile * 512 : tile * 512 + 512] = product_of(own_rows, ch, tile)
+
+    def shard(ch, o, part=slice(0, 4)):
         if ch < 2:
-            return rc(rs.at[ch, (x + j) % 4], r1.at[ch, j - 1], "rs1", ch * 4 + j, peer("x", j))
-        return rc(rs.at[ch, :, (y + j) % 4], r1.at[ch, j - 1], "rs1", ch * 4 + j, peer("y", j))
-
-    for ch in ORDER:
+            return rs.at[ch, (x + o) % 4, part]
+        return rs.at[ch, part, (y + o) % 4]
+
+    y_right = peer("y", 1)
+    y_left = peer("y", 3)
+
+    def q1_copies(ch):
+        r, l = (x_right, x_left) if ch < 2 else (y_right, y_left)
+        return (
+            rc(shard(ch, 2, slice(0, 2)), q1.at[ch, 0], "q1", ch * 2, r),
+            rc(shard(ch, 2, slice(2, 4)), q1.at[ch, 1], "q1", ch * 2 + 1, l),
+        )
+
+    def q2_copies(ch):
+        r, l = (x_right, x_left) if ch < 2 else (y_right, y_left)
+        return (
+            rc(shard(ch, 1), q2.at[ch, 0], "q2", ch * 2, r),
+            rc(shard(ch, 3), q2.at[ch, 1], "q2", ch * 2 + 1, l),
+        )
+
+    other_part(ORDER[0])
+    other_part(ORDER[1])
+    for i, ch in enumerate(ORDER):
+        own_part(ch)
+        if i + 2 < 4:
+            other_part(ORDER[i + 2])
         arrived(cr.at[ch], "core", ch)
         both = own[ch] + cr[ch].astype(f32)
         rs[ch] = both.astype(bf16).reshape(4, 4, 16, WIDE)
-        for j in range(1, 4):
-            rs1_copy(ch, j).start()
+        for cp in q1_copies(ch):
+            cp.start()
+    for ch in ORDER:
+        for cp in q1_copies(ch):
+            cp.wait_recv()
+        for o, part, way in ((1, slice(0, 2), 0), (3, slice(2, 4), 1)):
+            ref = shard(ch, o, part)
+            ref[...] = (ref[...].astype(f32) + q1[ch, way].astype(f32)).astype(bf16)
+        for cp in q2_copies(ch):
+            cp.start()
 
     ones = jnp.ones((8, SLICE), bf16)
 
@@ -422,10 +535,7 @@
     store_head = pltpu.make_async_copy(gh, ghead_hbm, ssem.at[BASE["load"] + 2])
     store_head.start()
     gain = cols[...]
-    for axis, buf in (("c", ga_c), ("x", ga_x)):
-        exchange(buf, "ga", axis, gain)
-        gain = functools.reduce(jnp.add, exchanged(buf, "ga", axis))
-    exchange(ga_y, "ga", "y", gain)
+    exchange(ga_cx, "ga", "cx", gain)
 
     def rs2_copy(ch, j):
         if ch < 2:
@@ -433,18 +543,16 @@
         return rc(s2.at[ch, (x + j) % 4], r2.at[ch, j - 1], "rs2", ch * 4 + j, peer("x", j))
 
     for ch in ORDER:
-        for j in range(1, 4):
-            arrived(r1.at[ch, j - 1], "rs1", ch * 4 + j)
-        kept = rs[ch, x] if ch < 2 else rs[ch, :, y]
-        total = kept.astype(f32)
-        for j in range(3):
-            total = total + r1[ch, j].astype(f32)
+        for cp in q2_copies(ch):
+            cp.wait_recv()
+        kept = shard(ch, 0)[...].astype(f32)
+        total = kept + (q2[ch, 0].astype(f32) + q2[ch, 1].astype(f32))
         s2[ch] = total.astype(bf16)
         for j in range(1, 4):
             rs2_copy(ch, j).start()
 
-    gain = functools.reduce(jnp.add, exchanged(ga_y, "ga", "y"))
-    exchange(ga_z, "ga", "z", gain)
+    gain = functools.reduce(jnp.add, exchanged(ga_cx, "ga", "cx"))
+    exchange(ga_y, "ga", "y", gain)
 
     for ch in ORDER:
         for j in range(1, 4):
@@ -454,33 +562,46 @@
         for j in range(3):
             total = total + r2[ch, j].astype(f32)
         for zz in range(8):
-            z3[zz, :, ch * WIDE : ch * WIDE + WIDE] = total[2 * zz : 2 * zz + 2, :]
+            for half in range(2):
+                at = 4 * ch + 2 * half
+                zf[zz, at : at + 2, :] = total[2 * zz : 2 * zz + 2, 512 * half : 512 * half + 512]
+    zb[...] = zf[...].astype(bf16)
 
     def rs3_copy(j):
-        return rc(z3.at[(z + j) % 8], r3.at[j - 1], "rs3", j, peer("z", j))
+        return rc(zb.at[(z + j) % 8], r3.at[j - 1], "rs3", j, peer("z", j))
 
     for j in range(1, 8):
         rs3_copy(j).start()
 
-    own_wide = sh_ref[...]
+    gain = functools.reduce(jnp.add, exchanged(ga_y, "ga", "y"))
+    exchange(ga_z, "ga", "z", gain)
+
+    own_wide = sh_ref[...].astype(f32)
     own_inv = lax.rsqrt(jnp.sum(own_wide * own_wide, -1, keepdims=True) / D_S + epsilon)
     own_normed = own_wide * own_inv
-    gain = functools.reduce(jnp.add, exchanged(ga_z, "ga", "z"))
-    ggain_ref[...] = gain / sg8_ref[...]
-
     for j in range(1, 8):
         arrived(r3.at[j - 1], "rs3", j)
-    grad_features = z3[z]
+    folded = zf[z]
     for j in range(7):
-        grad_features = grad_features + r3[j]
-    grad_normed = grad_features * sg_ref[...]
+        folded = folded + r3[j].astype(f32)
+    for i in range(8):
+        unfolded[:, 512 * i : 512 * i + 512] = folded[2 * i : 2 * i + 2, :]
+    grad_normed = unfolded[...] * gain_row
     inner = jnp.sum(grad_normed * own_normed, -1, keepdims=True) / D_S
     ghid_ref[...] = own_inv * (grad_normed - own_normed * inner)
+
+    gain = functools.reduce(jnp.add, exchanged(ga_z, "ga", "z"))
+    row = lax.broadcasted_iota(jnp.int32, (8, 512), 0)
+    gain_rows = jnp.ones((8, 512), f32)
+    for i in range(8):
+        gain_rows = jnp.where(row == i, gain_row[:, 512 * i : 512 * i + 512], gain_rows)
+    ggain_ref[...] = gain / gain_rows
 
     for buf, name in ((h5, "t"), (f5, "s")):
         yh_copy(buf, name).wait_send()
         for s in range(4):
-            for cp in ring_copies(buf, name, s):
+            copies = ring_copies(buf, name, s) if name == "t" else half_copies(s, 0) + half_copies(s, 1)
+            for cp in copies:
                 cp.wait_send()
         for s in range(5):
             for cp in sib_copies(buf, name, s):
@@ -489,18 +610,32 @@
         s0_copy(j).wait_send()
         sq_copy(j).wait_send()
         rs3_copy(j).wait_send()
-        for k in range(5):
-            part_copy(j, k).wait_send()
-    for name, bufs in (("st", (st_c, st_y, st_x, st_z)), ("ga", (ga_c, ga_y, ga_x, ga_z))):
-        for axis, buf in zip("cyxz", bufs):
+    for k in range(5):
+        for step in range(3):
+            for cp in ex_copies(k, step):
+                cp.wait_send()
+    for name, bufs in (("st", (st_cx, st_y, st_z)), ("ga", (ga_cx, ga_y, ga_z))):
+        for axis, buf in zip(("cx", "y", "z"), bufs):
             for j in range(1, size[axis]):
                 exchange_copy(buf, name, axis, j).wait_send()
     for ch in range(4):
         core_copy(ch).wait_send()
+        for cp in q1_copies(ch) + q2_copies(ch):
+            cp.wait_send()
         for j in range(1, 4):
-            rs1_copy(ch, j).wait_send()
             rs2_copy(ch, j).wait_send()
     store_head.wait()
+
+
+def finish(loss_ref, hidden_ref, gain_ref, head_ref, loss_out, hidden_out, gain_out, head_out):
+    head_out[...] = head_ref[...]
+
+    @pl.when(pl.program_id(0) == 0)
+    def _():
+        loss_out[...] = loss_ref[...]
+        hidden_out[...] = hidden_ref[...].astype(bf16)
+        for i in range(8):
+            gain_out[:, 512 * i : 512 * i + 512] = gain_ref[i : i + 1, :]
 
 
 def shards(
@@ -514,21 +649,27 @@
 ):
     vmem = pl.BlockSpec(memory_space=pltpu.VMEM)
     hbm = pl.BlockSpec(memory_space=pl.ANY)
-    gain_wide = student_gain.astype(f32)
+    block = pl.BlockSpec((1024, SLICE), lambda i: (i, 0))
+
+    def whole(*shape):
+        return pl.BlockSpec(shape, lambda i: (0, 0))
+
     row8 = (8, TOKENS)
     scratch = [
-        ((2048, 2048), bf16), ((D_S, SLICE), bf16), ((2, 8, 2, 16, 2048), bf16),
-        ((128, 2048), bf16), ((8, TOKENS, SLICE), f32), ((7, TOKENS, SLICE), f32),
+        ((2048, 2048), bf16), ((D_S, SLICE), bf16), ((SLICE, D_S), bf16), ((2, 8, 2, 16, 2048), bf16),
+        ((128, 2048), bf16), ((4, 2, 256, SLICE), f32), ((4, 2, 256, SLICE), f32),
+        ((4, 256, SLICE), f32), ((2, 256, SLICE), f32), ((2, 256, SLICE), f32),
+        ((2, 2, 256, SLICE), f32), ((2, 2, 256, SLICE), f32), ((256, SLICE), f32),
         ((2, 8, 32, 128), f32), (row8, f32), ((7,) + row8, f32),
         ((8, 2, D_S), f32), ((16, D_S), f32), ((2, 8, 2, 16, D_S), bf16),
         ((2, 8, 32, SLICE), f32), ((TOKENS, SLICE), f32), ((TOKENS, 128), f32), ((8, 512), f32),
-        ((2,) + row8, f32), ((4,) + row8, f32), ((4,) + row8, f32), ((8,) + row8, f32),
-        ((2,) + row8, f32), ((4,) + row8, f32), ((4,) + row8, f32), ((8,) + row8, f32),
-        ((TOKENS, SLICE), bf16), ((TOKENS, SLICE), bf16), ((D_S, SLICE), bf16),
+        ((8,) + row8, f32), ((4,) + row8, f32), ((8,) + row8, f32),
+        ((8,) + row8, f32), ((4,) + row8, f32), ((8,) + row8, f32),
+        ((TOKENS, SLICE), bf16), ((TOKENS, SLICE), bf16), ((TOKENS, TOKENS), bf16), ((D_S, SLICE), bf16),
         ((4, 256, WIDE), f32), ((4, 256, WIDE), bf16), ((4, 256, WIDE), bf16),
-        ((4, 4, 4, 16, WIDE), bf16), ((4, 3, 4, 16, WIDE), bf16),
+        ((4, 4, 4, 16, WIDE), bf16), ((4, 2, 2, 16, WIDE), bf16), ((4, 2, 4, 16, WIDE), bf16),
         ((4, 4, 16, WIDE), bf16), ((4, 3, 16, WIDE), bf16),
-        ((8, 2, D_S), f32), ((7, 2, D_S), f32),
+        ((8, 16, 512), f32), ((8, 16, 512), bf16), ((7, 16, 512), bf16), ((2, D_S), f32),
     ]
     loss, grad_head, grad_hidden, grad_gain = pl.pallas_call(
         kernel,
@@ -538,7 +679,7 @@
             jax.ShapeDtypeStruct((2, D_S), f32),
             jax.ShapeDtypeStruct((8, 512), f32),
         ),
-        in_specs=[vmem, vmem, hbm, vmem, vmem, vmem, hbm, vmem],
+        in_specs=[vmem, vmem, hbm, vmem, vmem, hbm, vmem],
         out_specs=(vmem, hbm, vmem, vmem),
         scratch_shapes=[pltpu.VMEM(shape, dtype) for shape, dtype in scratch]
         + [pltpu.SemaphoreType.DMA((N_SEMS,)), pltpu.SemaphoreType.DMA((N_SEMS,))],
@@ -550,20 +691,27 @@
         ),
     )(
         teacher_hidden,
-        teacher_gain.astype(f32).reshape(1, 2048),
+        teacher_gain,
         teacher_head,
-        student_hidden.astype(f32),
-        gain_wide.reshape(1, D_S),
-        gain_wide.reshape(8, 512),
+        student_hidden,
+        student_gain,
         student_head,
         token_ids.reshape(1, TOKENS),
     )
-    return (
-        loss.reshape(TOKENS),
-        grad_hidden.astype(bf16),
-        grad_gain.reshape(D_S),
-        grad_head,
-    )
+    loss, grad_hidden, grad_gain, grad_head = pl.pallas_call(
+        finish,
+        out_shape=(
+            jax.ShapeDtypeStruct((1, TOKENS), f32),
+            jax.ShapeDtypeStruct((2, D_S), bf16),
+            jax.ShapeDtypeStruct((1, D_S), f32),
+            jax.ShapeDtypeStruct((D_S, SLICE), bf16),
+        ),
+        grid=(4,),
+        in_specs=[whole(1, TOKENS), whole(2, D_S), whole(8, 512), block],
+        out_specs=(whole(1, TOKENS), whole(2, D_S), whole(1, D_S), block),
+        compiler_params=pltpu.CompilerParams(vmem_limit_bytes=56 * 1024 * 1024),
+    )(loss, grad_hidden, grad_gain, grad_head)
+    return loss.reshape(TOKENS), grad_hidden, grad_gain.reshape(D_S), grad_head
 
 
 def solution(mesh):

time: 135 us -> 115 us (0.85)
  Pallas kernels: 121 us -> 114 us
  local copies, waits for them, and re-layouts: 6.92 us -> 0 us
  other arithmetic: 5.31 us -> 0 us
    pallas_call x1, Pallas kernels: 121 us -> 110 us  [shards(): pl.pallas_call(kernel, out_shape=(jax.ShapeDtypeStruct((1, TOKENS), f32),...]
    unnamed x3 -> x0, local copies, waits for them, and re-layouts: 5.61 us -> none
    convert_element_type x3 -> x0, other arithmetic: 4.02 us -> none  [the longest x1 1.38 us: shards(): grad_hidden.astype(bf16)]
    pallas_call x0 -> x1, Pallas kernels: none -> 3.82 us  [shards(): pl.pallas_call(finish, out_shape=(jax.ShapeDtypeStruct((1, TOKENS), f32),...]
where the time goes in v2:
time: 115 us
  Pallas kernels  114 us (99%)
    pallas_call x1, Pallas kernels, shards(): pl.pallas_call(kernel, out_shape=(jax.ShapeDtypeStruct((1, TOKENS), f32),...  110 us
    pallas_call x1, Pallas kernels, shards(): pl.pallas_call(finish, out_shape=(jax.ShapeDtypeStruct((1, TOKENS), f32),...  3.82 us

profile of v2, /device:TPU:1, one launch (start us, length us, event | category | flops | bytes accessed | tf_op | source)
XLA Modules:
  0.0 115.0 jit_solution(1450671712685279142)
XLA Ops:
  0.6 110.5 %shard_map.102 = (f32[1,512]{1,0:T(1,128)}, bf16[4096,256]{1,0:T(8,128)(2,1)}, f32[2,4096]{1,0:T(2,128)}, f32[8,512]{1,0:T(8,128)}) custom-call(bf16[16,2048]{1,0:T(8,128)(2,1)} %th_ref.1, bf16[2048]{0:T(1024)(128)(2,1)} %tg_ref.1, bf16[2048,2048]{1,0:T(8,128)(2,1)} %thead_hbm.1, bf16[2,4096]{1,0:T(2,128)(2,1)} %sh_ref.1, bf16[4096]{0:T(1024)(128)(2,1)} %sg_ref.1, ...), custom_call_target="tpu_custom_call" | custom-call | flops 7600000000 | bytes 13000000 | tf_op jit(solution)/shard_map/pallas_call | solution.py:674
  111.1 3.8 %shard_map.103 = (f32[1,512]{1,0:T(1,128)}, bf16[2,4096]{1,0:T(2,128)(2,1)}, f32[1,4096]{1,0:T(1,128)}, bf16[4096,256]{1,0:T(8,128)(2,1)}) custom-call(f32[1,512]{1,0:T(1,128)} %get-tuple-element.12.loss_ref, f32[2,4096]{1,0:T(2,128)} %get-tuple-element.13.hidden_ref, f32[8,512]{1,0:T(8,128)} %get-tuple-element.14.gain_ref, ...), custom_call_target="tpu_custom_call" | custom-call | tf_op jit(solution)/shard_map/pallas_call | solution.py:701

commit v3 on v2

--- a/solution.py
+++ b/solution.py
@@ -19,7 +19,6 @@
 MESH = pl.DeviceIdType.MESH
 f32 = jnp.float32
 bf16 = jnp.bfloat16
-NT = (((1,), (1,)), ((), ()))
 
 CHUNK_ROWS = (32, 64, 64, 64, 32)
 CHUNK_AT = (0, 32, 96, 160, 224)
@@ -60,9 +59,9 @@
     th_ref, tg_ref, thead_hbm, sh_ref, sg_ref, shead_hbm, ids_ref,
     loss_ref, ghead_hbm, ghid_ref, ggain_ref,
     head, w, wt, h5, scaled, pa, pb, ya, xa1, xa2, xb1, xb2, yb, ssq, sqs, sqr,
-    s0, s16, f5, t4, slog, stc, cols,
+    s0, s16, f5, t4, slog, stc, cols, idc,
     st_cx, st_y, st_z, ga_cx, ga_y, ga_z,
-    g_s, gp, perm, gh, own, cs, cr, rs, q1, q2, s2, r2, zf, zb, r3, unfolded,
+    gp, perm, gh, own, cs, cr, rs, q1, q2, s2, r2, zf, zb, r3, unfolded,
     ssem, rsem,
 ):
     tp = lax.axis_index("tp")
@@ -107,8 +106,8 @@
 
     load_head = pltpu.make_async_copy(thead_hbm, head, ssem.at[BASE["load"]])
     load_w = pltpu.make_async_copy(shead_hbm, w, ssem.at[BASE["load"] + 1])
+    load_w.start()
     load_head.start()
-    load_w.start()
 
     barrier = pltpu.get_barrier_semaphore()
     partners = [peer("c", 1)]
@@ -121,6 +120,20 @@
 
     h5[yh, z, c] = th_ref[...]
     s0[dp] = sh_ref[...].astype(f32)
+    idc[...] = jnp.broadcast_to(ids_ref[...], (128, TOKENS)).T
+
+    p = lax.broadcasted_iota(jnp.int32, (TOKENS, TOKENS), 0)
+    q = lax.broadcasted_iota(jnp.int32, (TOKENS, TOKENS), 1)
+    source = (
+        ((p >> 5) & 1) * 256
+        + ((p >> 1) & 7) * 32
+        + (p >> 8) * 16
+        + ((p >> 6) & 3) * 4
+        + ((p >> 4) & 1) * 2
+        + (p & 1)
+    )
+    perm[...] = jnp.where(q == source, 1.0, 0.0).astype(bf16)
+
     pl.semaphore_wait(barrier, len(partners))
 
     yh_peer = dev(x, (y + 2) % 4, z, c)
@@ -197,6 +210,14 @@
     for j in range(1, 8):
         s0_copy(j).start()
 
+    load_w.wait()
+
+    def turn(i, carry):
+        at = pl.ds(pl.multiple_of(i * 512, 512), 512)
+        wt[:, at] = w[at, :].T
+        return carry
+
+    lax.fori_loop(0, 8, turn, 0)
     arrived(h5.at[1 - yh, z, c], "t_yh", 0)
     for cp in ring_copies(h5, "t", 0):
         cp.start()
@@ -223,7 +244,7 @@
         at, n = CHUNK_AT[k], CHUNK_ROWS[k]
         return {"all": pl.ds(at, n), "r": pl.ds(at, n // 2), "l": pl.ds(at + n // 2, n // 2)}[part]
 
-    def ex_copies(k, step):
+    def ex_copies(k, step, which="ab"):
         every, rows_r, rows_l = span(k, "all"), span(k, "r"), span(k, "l")
         a_y = (pa.at[:, 1, every], ya.at[:, every], 0, y_pair)
         a_x1r = (pa.at[2, 0, rows_r], xa1.at[0, rows_r], 1, x_right)
@@ -235,34 +256,43 @@
         b_x2r = (pb.at[1, :, every], xb2.at[0, :, every], 7, x_right)
         b_x2l = (pb.at[3, :, every], xb2.at[1, :, every], 8, x_left)
         b_y = (pb.at[0, 1, every], yb.at[every], 9, y_pair)
-        steps = (
-            (a_y, b_x1r, b_x1l), (a_x1r, a_x1l, b_x2r, b_x2l), (a_x2r, a_x2l, b_y),
-        )
-        return [rc(src, dst, "ex", k * 10 + i, device) for src, dst, i, device in steps[step]]
-
-    def ex_arrived(k, step):
-        for cp in ex_copies(k, step):
+        steps = {
+            "a": ((a_y,), (a_x1r, a_x1l), (a_x2r, a_x2l)),
+            "b": ((b_x1r, b_x1l), (b_x2r, b_x2l), (b_y,)),
+        }
+        return [
+            rc(src, dst, "ex", k * 10 + i, device)
+            for part in which
+            for src, dst, i, device in steps[part][step]
+        ]
+
+    def ex_arrived(k, step, which="ab"):
+        for cp in ex_copies(k, step, which):
             cp.wait_recv()
 
-    def ex_send(k, step):
-        for cp in ex_copies(k, step):
+    def ex_send(k, step, which):
+        for cp in ex_copies(k, step, which):
             cp.start()
 
     def ex_second(k):
         every, rows_r, rows_l = span(k, "all"), span(k, "r"), span(k, "l")
-        ex_arrived(k, 0)
+        ex_arrived(k, 0, "b")
         pb[1, :, rows_r] += xb1[0, :, rows_r]
         pb[3, :, rows_l] += xb1[1, :, rows_l]
+        ex_send(k, 1, "b")
+        ex_arrived(k, 0, "a")
         pa[:, 0, every] += ya[:, every]
-        ex_send(k, 1)
+        ex_send(k, 1, "a")
 
     def ex_third(k):
         every, rows_r, rows_l = span(k, "all"), span(k, "r"), span(k, "l")
-        ex_arrived(k, 1)
+        ex_arrived(k, 1, "b")
+        pb[0, :, every] += xb2[0, :, every] + xb2[1, :, every]
+        ex_send(k, 2, "b")
+        ex_arrived(k, 1, "a")
         pa[1, 0, rows_r] += xa1[0, rows_r]
         pa[3, 0, rows_l] += xa1[1, rows_l]
-        pb[0, :, every] += xb2[0, :, every] + xb2[1, :, every]
-        ex_send(k, 2)
+        ex_send(k, 2, "a")
 
     def teacher_chunk(k):
         for i, (_, zz) in enumerate(units(k)):
@@ -277,26 +307,24 @@
                 scaled[at : at + 32, :] = (block * tg).astype(bf16)
         m = CHUNK_ROWS[k]
 
-        def product(j, carry):
-            xo, yo = j // 2, j % 2
+        def product(xo, yo):
             d = ((x + xo) % 4) * 2 + (yl + yo) % 2
             columns = pl.ds(pl.multiple_of(d * SLICE, SLICE), SLICE)
             both = jnp.dot(scaled[0 : 2 * m, :], head[:, columns], preferred_element_type=f32)
             pa[xo, yo, CHUNK_AT[k] : CHUNK_AT[k] + m, :] = both[0:m]
             pb[xo, yo, CHUNK_AT[k] : CHUNK_AT[k] + m, :] = both[m : 2 * m]
+
+        def other_y(xo, carry):
+            product(xo, 1)
             return carry
 
-        lax.fori_loop(0, 8, product, 0)
-        ex_send(k, 0)
-
-    load_w.wait()
-
-    def turn(i, carry):
-        at = pl.ds(pl.multiple_of(i * 512, 512), 512)
-        wt[:, at] = w[at, :].T
-        return carry
-
-    lax.fori_loop(0, 8, turn, 0)
+        lax.fori_loop(0, 4, other_y, 0)
+        ex_send(k, 0, "a")
+        product(2, 0)
+        ex_send(k, 0, "b")
+        for xo in (1, 3, 0):
+            product(xo, 0)
+
     load_head.wait()
     for s in range(4):
         ring_arrived(h5, "t", s)
@@ -305,6 +333,10 @@
                 cp.start()
         for cp in sib_copies(h5, "t", s + 1):
             cp.start()
+        if s >= 2:
+            student_step(0, s - 2)
+        sib_arrived(h5, "t", s)
+        teacher_chunk(s)
         if s == 0:
             arrived(f5.at[1 - yh, z, c], "s_yh", 0)
             for half in range(2):
@@ -312,10 +344,6 @@
                     cp.start()
             for cp in sib_copies(f5, "s", 0):
                 cp.start()
-        if s >= 2:
-            student_step(0, s - 2)
-        sib_arrived(h5, "t", s)
-        teacher_chunk(s)
         if s >= 1:
             ex_second(s - 1)
         if s >= 2:
@@ -346,25 +374,10 @@
     for s in range(5):
         sib_arrived(f5, "s", s)
 
-    p = lax.broadcasted_iota(jnp.int32, (TOKENS, TOKENS), 0)
-    q = lax.broadcasted_iota(jnp.int32, (TOKENS, TOKENS), 1)
-    source = (
-        ((p >> 5) & 1) * 256
-        + ((p >> 1) & 7) * 32
-        + (p >> 8) * 16
-        + ((p >> 6) & 3) * 4
-        + ((p >> 4) & 1) * 2
-        + (p & 1)
-    )
-    perm[...] = jnp.where(q == source, 1.0, 0.0).astype(bf16)
-
     for half in range(2):
-        for quarter in range(2):
-            rows = f5[half, 4 * quarter : 4 * quarter + 4].reshape(128, D_S)
-            at = half * 256 + quarter * 128
-            slog[at : at + 128, :] = jnp.dot(rows, w[...], preferred_element_type=f32)
-    ids = jnp.broadcast_to(ids_ref[...], (128, TOKENS)).T
-    ids = jnp.concatenate([ids, ids], axis=1)
+        rows = f5[half].reshape(256, D_S)
+        slog[half * 256 : half * 256 + 256, :] = jnp.dot(rows, w[...], preferred_element_type=f32)
+    ids = jnp.concatenate([idc[...], idc[...]], axis=1)
     first = (tp * 8 + dp) * SLICE
     target_mask = ids == first + lax.broadcasted_iota(jnp.int32, (TOKENS, SLICE), 1)
     student = slog[...]
@@ -448,7 +461,6 @@
     s_prob = jnp.exp(student - jnp.concatenate([s_col, s_col], axis=1))
     onehot = target_mask.astype(f32)
     g = (loss_scale * (s_prob - t_prob + hard_weight * (s_prob - onehot))).astype(bf16)
-    g_s[...] = g
 
     gp[...] = jnp.dot(perm[...], g, preferred_element_type=f32).astype(bf16)
 
@@ -512,25 +524,16 @@
         for cp in q2_copies(ch):
             cp.start()
 
-    ones = jnp.ones((8, SLICE), bf16)
+    turned = g.T
 
     def head_tile(i, carry):
         at = pl.ds(pl.multiple_of(i * 512, 512), 512)
         features = f5[:, :, :, :, at].reshape(TOKENS, 512)
-        tile = jnp.dot(features.T, g_s[...], preferred_element_type=f32)
-        gh[at, :] = tile.astype(bf16)
-        product = tile * w[at, :].astype(f32)
-        high = product.astype(bf16)
-        low = (product - high.astype(f32)).astype(bf16)
-        row = lax.dot_general(ones, high, NT, preferred_element_type=f32) + lax.dot_general(
-            ones, low, NT, preferred_element_type=f32
-        )
-        cols[...] = jnp.where(
-            lax.broadcasted_iota(jnp.int32, (8, 512), 0) == i, row, cols[...]
-        )
+        tile = jnp.dot(turned, features, preferred_element_type=f32)
+        cols[pl.ds(i, 1), :] = jnp.sum(tile * wt[:, at].astype(f32), 0, keepdims=True)
+        gh[at, :] = tile.astype(bf16).T
         return carry
 
-    cols[...] = jnp.zeros((8, 512), f32)
     lax.fori_loop(0, 8, head_tile, 0)
     store_head = pltpu.make_async_copy(gh, ghead_hbm, ssem.at[BASE["load"] + 2])
     store_head.start()
@@ -649,7 +652,7 @@
 ):
     vmem = pl.BlockSpec(memory_space=pltpu.VMEM)
     hbm = pl.BlockSpec(memory_space=pl.ANY)
-    block = pl.BlockSpec((1024, SLICE), lambda i: (i, 0))
+    block = pl.BlockSpec((2048, SLICE), lambda i: (i, 0))
 
     def whole(*shape):
         return pl.BlockSpec(shape, lambda i: (0, 0))
@@ -663,9 +666,10 @@
         ((2, 8, 32, 128), f32), (row8, f32), ((7,) + row8, f32),
         ((8, 2, D_S), f32), ((16, D_S), f32), ((2, 8, 2, 16, D_S), bf16),
         ((2, 8, 32, SLICE), f32), ((TOKENS, SLICE), f32), ((TOKENS, 128), f32), ((8, 512), f32),
+        ((TOKENS, 128), jnp.int32),
         ((8,) + row8, f32), ((4,) + row8, f32), ((8,) + row8, f32),
         ((8,) + row8, f32), ((4,) + row8, f32), ((8,) + row8, f32),
-        ((TOKENS, SLICE), bf16), ((TOKENS, SLICE), bf16), ((TOKENS, TOKENS), bf16), ((D_S, SLICE), bf16),
+        ((TOKENS, SLICE), bf16), ((TOKENS, TOKENS), bf16), ((D_S, SLICE), bf16),
         ((4, 256, WIDE), f32), ((4, 256, WIDE), bf16), ((4, 256, WIDE), bf16),
         ((4, 4, 4, 16, WIDE), bf16), ((4, 2, 2, 16, WIDE), bf16), ((4, 2, 4, 16, WIDE), bf16),
         ((4, 4, 16, WIDE), bf16), ((4, 3, 16, WIDE), bf16),
@@ -706,7 +710,7 @@
             jax.ShapeDtypeStruct((1, D_S), f32),
             jax.ShapeDtypeStruct((D_S, SLICE), bf16),
         ),
-        grid=(4,),
+        grid=(2,),
         in_specs=[whole(1, TOKENS), whole(2, D_S), whole(8, 512), block],
         out_specs=(whole(1, TOKENS), whole(2, D_S), whole(1, D_S), block),
         compiler_params=pltpu.CompilerParams(vmem_limit_bytes=56 * 1024 * 1024),

time: 115 us -> 113 us (0.983)
    pallas_call x1, Pallas kernels: 3.82 us -> 2.66 us  [shards(): pl.pallas_call(finish, out_shape=(jax.ShapeDtypeStruct((1, TOKENS), f32),...]
where the time goes in v3:
time: 113 us
  Pallas kernels  113 us (100%)
    pallas_call x1, Pallas kernels, shards(): pl.pallas_call(kernel, out_shape=(jax.ShapeDtypeStruct((1, TOKENS), f32),...  110 us
    pallas_call x1, Pallas kernels, shards(): pl.pallas_call(finish, out_shape=(jax.ShapeDtypeStruct((1, TOKENS), f32),...  2.66 us

profile of v3, /device:TPU:1, one launch (start us, length us, event | category | flops | bytes accessed | tf_op | source)
XLA Modules:
  0.0 113.2 jit_solution(12755587690865166489)
XLA Ops:
  0.6 109.9 %shard_map.102 = (f32[1,512]{1,0:T(1,128)}, bf16[4096,256]{1,0:T(8,128)(2,1)}, f32[2,4096]{1,0:T(2,128)}, f32[8,512]{1,0:T(8,128)}) custom-call(bf16[16,2048]{1,0:T(8,128)(2,1)} %th_ref.1, bf16[2048]{0:T(1024)(128)(2,1)} %tg_ref.1, bf16[2048,2048]{1,0:T(8,128)(2,1)} %thead_hbm.1, bf16[2,4096]{1,0:T(2,128)(2,1)} %sh_ref.1, bf16[4096]{0:T(1024)(128)(2,1)} %sg_ref.1, ...), custom_call_target="tpu_custom_call" | custom-call | flops 7600000000 | bytes 13000000 | tf_op jit(solution)/shard_map/pallas_call | solution.py:678
  110.6 2.7 %shard_map.103 = (f32[1,512]{1,0:T(1,128)}, bf16[2,4096]{1,0:T(2,128)(2,1)}, f32[1,4096]{1,0:T(1,128)}, bf16[4096,256]{1,0:T(8,128)(2,1)}) custom-call(f32[1,512]{1,0:T(1,128)} %get-tuple-element.12.loss_ref, f32[2,4096]{1,0:T(2,128)} %get-tuple-element.13.hidden_ref, f32[8,512]{1,0:T(8,128)} %get-tuple-element.14.gain_ref, ...), custom_call_target="tpu_custom_call" | custom-call | tf_op jit(solution)/shard_map/pallas_call | solution.py:705

commit v4 on v3

--- a/solution.py
+++ b/solution.py
@@ -46,7 +46,7 @@
         ("s0", 8), ("ex", 50), ("sq", 8),
         ("st_cx", 8), ("st_y", 4), ("st_z", 8),
         ("ga_cx", 8), ("ga_y", 4), ("ga_z", 8),
-        ("core", 4), ("q1", 8), ("q2", 8), ("rs2", 16), ("rs3", 8),
+        ("wt", 1), ("gp", 1), ("q1", 8), ("q2", 8), ("rs2", 16), ("rs3", 8),
     ):
         base[name] = s.take(n)
     return base, s.count
@@ -59,9 +59,9 @@
     th_ref, tg_ref, thead_hbm, sh_ref, sg_ref, shead_hbm, ids_ref,
     loss_ref, ghead_hbm, ghid_ref, ggain_ref,
     head, w, wt, h5, scaled, pa, pb, ya, xa1, xa2, xb1, xb2, yb, ssq, sqs, sqr,
-    s0, s16, f5, t4, slog, stc, cols, idc,
+    s0, s16, f5, t4, slog, cols,
     st_cx, st_y, st_z, ga_cx, ga_y, ga_z,
-    gp, perm, gh, own, cs, cr, rs, q1, q2, s2, r2, zf, zb, r3, unfolded,
+    gp, gr, perm, gh, rs, q1, q2, s2, r2, zf, zb, r3, unfolded,
     ssem, rsem,
 ):
     tp = lax.axis_index("tp")
@@ -120,10 +120,9 @@
 
     h5[yh, z, c] = th_ref[...]
     s0[dp] = sh_ref[...].astype(f32)
-    idc[...] = jnp.broadcast_to(ids_ref[...], (128, TOKENS)).T
-
-    p = lax.broadcasted_iota(jnp.int32, (TOKENS, TOKENS), 0)
-    q = lax.broadcasted_iota(jnp.int32, (TOKENS, TOKENS), 1)
+
+    p = lax.broadcasted_iota(jnp.int32, (TOKENS, TOKENS), 1)
+    q = lax.broadcasted_iota(jnp.int32, (TOKENS, TOKENS), 0)
     source = (
         ((p >> 5) & 1) * 256
         + ((p >> 1) & 7) * 32
@@ -214,7 +213,7 @@
 
     def turn(i, carry):
         at = pl.ds(pl.multiple_of(i * 512, 512), 512)
-        wt[:, at] = w[at, :].T
+        wt[0:SLICE, at] = w[at, :].T
         return carry
 
     lax.fori_loop(0, 8, turn, 0)
@@ -351,10 +350,22 @@
     student_step(1, 0)
     sib_arrived(h5, "t", 4)
     teacher_chunk(4)
+    wt_copy = rc(wt.at[0:SLICE], wt.at[SLICE : 2 * SLICE], "wt", 0, sibling)
+    wt_copy.start()
     student_step(1, 1)
 
-    sums = jnp.sum(ssq[...].reshape(TOKENS, 128).T, 0, keepdims=True)
-    sqs[...] = jnp.broadcast_to(sums, (8, TOKENS))
+    def fold(*rows):
+        pieces = [v[:, 128 * i : 128 * i + 128] for v in rows for i in range(4)]
+        row = lax.broadcasted_iota(jnp.int32, (8, 128), 0)
+        out = jnp.zeros((8, 128), f32)
+        for i, piece in enumerate(pieces):
+            out = jnp.where(row == i, piece, out)
+        return out
+
+    def unfold(tile, first):
+        return jnp.concatenate([tile[first + i : first + i + 1, :] for i in range(4)], axis=1)
+
+    sqs[...] = fold(jnp.sum(ssq[...].reshape(TOKENS, 128).T, 0, keepdims=True))
 
     def sq_copy(j):
         return rc(sqs, sqr.at[j - 1], "sq", j, (tp, (dp + j) % 8))
@@ -376,46 +387,42 @@
 
     for half in range(2):
         rows = f5[half].reshape(256, D_S)
-        slog[half * 256 : half * 256 + 256, :] = jnp.dot(rows, w[...], preferred_element_type=f32)
-    ids = jnp.concatenate([idc[...], idc[...]], axis=1)
+        slog[:, half * 256 : half * 256 + 256] = jnp.dot(
+            rows, w[...], preferred_element_type=f32
+        ).T
     first = (tp * 8 + dp) * SLICE
-    target_mask = ids == first + lax.broadcasted_iota(jnp.int32, (TOKENS, SLICE), 1)
+    target_mask = ids_ref[...] == first + lax.broadcasted_iota(jnp.int32, (SLICE, TOKENS), 0)
     student = slog[...]
-    s_top = jnp.max(student, -1, keepdims=True)
-    s_total = jnp.sum(jnp.exp(student - s_top), -1, keepdims=True)
-    target = jnp.sum(jnp.where(target_mask, student, 0.0), -1, keepdims=True)
-    lane = lax.broadcasted_iota(jnp.int32, (TOKENS, 128), 1)
-    stc[...] = jnp.where(
-        lane == 3, s_top, jnp.where(lane == 4, s_total, jnp.where(lane == 5, target, 0.0))
-    )
+    s_top = jnp.max(student, 0, keepdims=True)
+    s_total = jnp.sum(jnp.exp(student - s_top), 0, keepdims=True)
+    target = jnp.sum(jnp.where(target_mask, student, 0.0), 0, keepdims=True)
 
     for j in range(1, 8):
         arrived(sqr.at[j - 1], "sq", j)
     square_total = sqs[...]
     for j in range(7):
         square_total = square_total + sqr[j]
-    t_inv = lax.rsqrt(square_total / D_T + epsilon)
-    t_inv = jnp.broadcast_to(t_inv[0:1, :], (128, TOKENS)).T
-    t_inv = jnp.concatenate([t_inv, t_inv], axis=1)
+    t_inv = unfold(lax.rsqrt(square_total / D_T + epsilon), 0)
     for k in range(5):
         ex_arrived(k, 2)
         for i, (_, zz) in enumerate(units(k)):
             rows = pl.ds(CHUNK_AT[k] + 32 * i, 32)
             t4[0, zz] = pa[0, 0, rows] + xa2[0, rows] + xa2[1, rows]
             t4[1, zz] = pb[0, 0, rows] + yb[rows]
-    teacher = t4[...].reshape(TOKENS, SLICE) * t_inv
-
-    t_top = jnp.max(teacher, -1, keepdims=True)
+    teacher = t4[...].reshape(TOKENS, SLICE).T * t_inv
+
+    t_top = jnp.max(teacher, 0, keepdims=True)
     t_exp = jnp.exp(teacher - t_top)
-    t_total = jnp.sum(t_exp, -1, keepdims=True)
-    cross = jnp.sum(t_exp * (teacher - student), -1, keepdims=True)
-    packed = jnp.where(
-        lane == 0, t_top, jnp.where(lane == 1, t_total, jnp.where(lane == 2, cross, stc[...]))
-    )
-    stats = packed.T[0:8, :]
+    t_total = jnp.sum(t_exp, 0, keepdims=True)
+    cross = jnp.sum(t_exp * (teacher - student), 0, keepdims=True)
+    stats = (fold(t_top, s_top), fold(t_total, s_total), fold(cross, target))
 
     def exchange(buf, name, axis, value):
-        buf[mine[axis]] = value
+        if isinstance(value, tuple):
+            for i, v in enumerate(value):
+                buf[mine[axis], i] = v
+        else:
+            buf[mine[axis]] = value
         for j in range(1, size[axis]):
             exchange_copy(buf, name, axis, j).start()
 
@@ -429,58 +436,37 @@
             arrived(buf.at[(mine[axis] + n - j) % n], name + "_" + axis, j)
         return [buf[i] for i in range(n)]
 
+    upper = lax.broadcasted_iota(jnp.int32, (8, 128), 0) < 4
+
     def merged(parts):
-        t_m = functools.reduce(jnp.maximum, [p[0:1] for p in parts])
-        s_m = functools.reduce(jnp.maximum, [p[3:4] for p in parts])
-        t_s = c_s = s_s = tgt = 0.0
+        top = functools.reduce(jnp.maximum, [p[0] for p in parts])
+        total = other = 0.0
         for p in parts:
-            t_f = jnp.exp(p[0:1] - t_m)
-            s_f = jnp.exp(p[3:4] - s_m)
-            t_s = t_s + p[1:2] * t_f
-            c_s = c_s + p[2:3] * t_f
-            s_s = s_s + p[4:5] * s_f
-            tgt = tgt + p[5:6]
-        row = lax.broadcasted_iota(jnp.int32, (8, TOKENS), 0)
-        out = jnp.zeros((8, TOKENS), f32)
-        for i, v in enumerate((t_m, t_s, c_s, s_m, s_s, tgt)):
-            out = jnp.where(row == i, v, out)
-        return out
+            factor = jnp.exp(p[0] - top)
+            total = total + p[1] * factor
+            other = other + p[2] * jnp.where(upper, factor, 1.0)
+        return top, total, other
 
     for axis, buf in (("cx", st_cx), ("y", st_y), ("z", st_z)):
         exchange(buf, "st", axis, stats)
         stats = merged(exchanged(buf, "st", axis))
 
-    t_lse = stats[0:1] + jnp.log(stats[1:2])
-    s_lse = stats[3:4] + jnp.log(stats[4:5])
-    loss_ref[...] = (
-        stats[2:3] / stats[1:2] - t_lse + s_lse + hard_weight * (s_lse - stats[5:6])
-    )
-    t_col = jnp.broadcast_to(t_lse, (128, TOKENS)).T
-    s_col = jnp.broadcast_to(s_lse, (128, TOKENS)).T
-    t_prob = jnp.exp(teacher - jnp.concatenate([t_col, t_col], axis=1))
-    s_prob = jnp.exp(student - jnp.concatenate([s_col, s_col], axis=1))
+    top, total, other = stats
+    lse = top + jnp.log(total)
+    t_lse, s_lse = unfold(lse, 0), unfold(lse, 4)
+    cross_mean, target = unfold(other / total, 0), unfold(other, 4)
+    loss_ref[...] = cross_mean - t_lse + s_lse + hard_weight * (s_lse - target)
+    t_prob = jnp.exp(teacher - t_lse)
+    s_prob = jnp.exp(student - s_lse)
     onehot = target_mask.astype(f32)
     g = (loss_scale * (s_prob - t_prob + hard_weight * (s_prob - onehot))).astype(bf16)
 
-    gp[...] = jnp.dot(perm[...], g, preferred_element_type=f32).astype(bf16)
-
-    def core_copy(ch):
-        return rc(cs.at[ch], cr.at[ch], "core", ch, sibling)
+    gp[...] = jnp.dot(g, perm[...], preferred_element_type=f32).astype(bf16).T
 
     other_rows = pl.ds(pl.multiple_of((1 - c) * 256, 256), 256)
     own_rows = pl.ds(pl.multiple_of(c * 256, 256), 256)
-    def product_of(rows, ch, tile):
-        at = ch * WIDE + tile * 512
-        return jnp.dot(gp[rows, :], wt[:, at : at + 512], preferred_element_type=f32)
-
-    def other_part(ch):
-        for tile in range(2):
-            cs[ch, :, tile * 512 : tile * 512 + 512] = product_of(other_rows, ch, tile).astype(bf16)
-        core_copy(ch).start()
-
-    def own_part(ch):
-        for tile in range(2):
-            own[ch, :, tile * 512 : tile * 512 + 512] = product_of(own_rows, ch, tile)
+    gp_copy = rc(gp.at[other_rows], gr, "gp", 0, sibling)
+    gp_copy.start()
 
     def shard(ch, o, part=slice(0, 4)):
         if ch < 2:
@@ -504,15 +490,16 @@
             rc(shard(ch, 3), q2.at[ch, 1], "q2", ch * 2 + 1, l),
         )
 
-    other_part(ORDER[0])
-    other_part(ORDER[1])
-    for i, ch in enumerate(ORDER):
-        own_part(ch)
-        if i + 2 < 4:
-            other_part(ORDER[i + 2])
-        arrived(cr.at[ch], "core", ch)
-        both = own[ch] + cr[ch].astype(f32)
-        rs[ch] = both.astype(bf16).reshape(4, 4, 16, WIDE)
+    arrived(wt.at[SLICE : 2 * SLICE], "wt", 0)
+    arrived(gr, "gp", 0)
+    both_slices = jnp.concatenate([gp[own_rows, :], gr[...]], axis=1)
+    for ch in ORDER:
+        for tile in range(2):
+            at = ch * WIDE + tile * 512
+            product = jnp.dot(both_slices, wt[:, at : at + 512], preferred_element_type=f32)
+            rs[ch, :, :, :, tile * 512 : tile * 512 + 512] = product.astype(bf16).reshape(
+                4, 4, 16, 512
+            )
         for cp in q1_copies(ch):
             cp.start()
     for ch in ORDER:
@@ -524,13 +511,11 @@
         for cp in q2_copies(ch):
             cp.start()
 
-    turned = g.T
-
     def head_tile(i, carry):
         at = pl.ds(pl.multiple_of(i * 512, 512), 512)
         features = f5[:, :, :, :, at].reshape(TOKENS, 512)
-        tile = jnp.dot(turned, features, preferred_element_type=f32)
-        cols[pl.ds(i, 1), :] = jnp.sum(tile * wt[:, at].astype(f32), 0, keepdims=True)
+        tile = jnp.dot(g, features, preferred_element_type=f32)
+        cols[pl.ds(i, 1), :] = jnp.sum(tile * wt[0:SLICE, at].astype(f32), 0, keepdims=True)
         gh[at, :] = tile.astype(bf16).T
         return carry
 
@@ -622,11 +607,12 @@
             for j in range(1, size[axis]):
                 exchange_copy(buf, name, axis, j).wait_send()
     for ch in range(4):
-        core_copy(ch).wait_send()
         for cp in q1_copies(ch) + q2_copies(ch):
             cp.wait_send()
         for j in range(1, 4):
             rs2_copy(ch, j).wait_send()
+    wt_copy.wait_send()
+    gp_copy.wait_send()
     store_head.wait()
 
 
@@ -659,18 +645,16 @@
 
     row8 = (8, TOKENS)
     scratch = [
-        ((2048, 2048), bf16), ((D_S, SLICE), bf16), ((SLICE, D_S), bf16), ((2, 8, 2, 16, 2048), bf16),
+        ((2048, 2048), bf16), ((D_S, SLICE), bf16), ((2 * SLICE, D_S), bf16), ((2, 8, 2, 16, 2048), bf16),
         ((128, 2048), bf16), ((4, 2, 256, SLICE), f32), ((4, 2, 256, SLICE), f32),
         ((4, 256, SLICE), f32), ((2, 256, SLICE), f32), ((2, 256, SLICE), f32),
         ((2, 2, 256, SLICE), f32), ((2, 2, 256, SLICE), f32), ((256, SLICE), f32),
-        ((2, 8, 32, 128), f32), (row8, f32), ((7,) + row8, f32),
+        ((2, 8, 32, 128), f32), ((8, 128), f32), ((7, 8, 128), f32),
         ((8, 2, D_S), f32), ((16, D_S), f32), ((2, 8, 2, 16, D_S), bf16),
-        ((2, 8, 32, SLICE), f32), ((TOKENS, SLICE), f32), ((TOKENS, 128), f32), ((8, 512), f32),
-        ((TOKENS, 128), jnp.int32),
+        ((2, 8, 32, SLICE), f32), ((SLICE, TOKENS), f32), ((8, 512), f32),
+        ((8, 3, 8, 128), f32), ((4, 3, 8, 128), f32), ((8, 3, 8, 128), f32),
         ((8,) + row8, f32), ((4,) + row8, f32), ((8,) + row8, f32),
-        ((8,) + row8, f32), ((4,) + row8, f32), ((8,) + row8, f32),
-        ((TOKENS, SLICE), bf16), ((TOKENS, TOKENS), bf16), ((D_S, SLICE), bf16),
-        ((4, 256, WIDE), f32), ((4, 256, WIDE), bf16), ((4, 256, WIDE), bf16),
+        ((TOKENS, SLICE), bf16), ((256, SLICE), bf16), ((TOKENS, TOKENS), bf16), ((D_S, SLICE), bf16),
         ((4, 4, 4, 16, WIDE), bf16), ((4, 2, 2, 16, WIDE), bf16), ((4, 2, 4, 16, WIDE), bf16),
         ((4, 4, 16, WIDE), bf16), ((4, 3, 16, WIDE), bf16),
         ((8, 16, 512), f32), ((8, 16, 512), bf16), ((7, 16, 512), bf16), ((2, D_S), f32),

time: 113 us -> 110 us (0.973)
  Pallas kernels: 113 us -> 109 us
    pallas_call x1, Pallas kernels: 110 us -> 106 us  [shards(): pl.pallas_call(kernel, out_shape=(jax.ShapeDtypeStruct((1, TOKENS), f32),...]
where the time goes in v4:
time: 110 us
  Pallas kernels  109 us (99%)
    pallas_call x1, Pallas kernels, shards(): pl.pallas_call(kernel, out_shape=(jax.ShapeDtypeStruct((1, TOKENS), f32),...  106 us
    pallas_call x1, Pallas kernels, shards(): pl.pallas_call(finish, out_shape=(jax.ShapeDtypeStruct((1, TOKENS), f32),...  2.66 us

profile of v4, /device:TPU:1, one launch (start us, length us, event | category | flops | bytes accessed | tf_op | source)
XLA Modules:
  0.0 109.6 jit_solution(13290260159193304892)
XLA Ops:
  0.6 106.3 %shard_map.102 = (f32[1,512]{1,0:T(1,128)}, bf16[4096,256]{1,0:T(8,128)(2,1)}, f32[2,4096]{1,0:T(2,128)}, f32[8,512]{1,0:T(8,128)}) custom-call(bf16[16,2048]{1,0:T(8,128)(2,1)} %th_ref.1, bf16[2048]{0:T(1024)(128)(2,1)} %tg_ref.1, bf16[2048,2048]{1,0:T(8,128)(2,1)} %thead_hbm.1, bf16[2,4096]{1,0:T(2,128)(2,1)} %sh_ref.1, bf16[4096]{0:T(1024)(128)(2,1)} %sg_ref.1, ...), custom_call_target="tpu_custom_call" | custom-call | flops 7600000000 | bytes 13000000 | tf_op jit(solution)/shard_map/pallas_call | solution.py:662
  106.9 2.7 %shard_map.103 = (f32[1,512]{1,0:T(1,128)}, bf16[2,4096]{1,0:T(2,128)(2,1)}, f32[1,4096]{1,0:T(1,128)}, bf16[4096,256]{1,0:T(8,128)(2,1)}) custom-call(f32[1,512]{1,0:T(1,128)} %get-tuple-element.12.loss_ref, f32[2,4096]{1,0:T(2,128)} %get-tuple-element.13.hidden_ref, f32[8,512]{1,0:T(8,128)} %get-tuple-element.14.gain_ref, ...), custom_call_target="tpu_custom_call" | custom-call | tf_op jit(solution)/shard_map/pallas_call | solution.py:689

commit v5 on v4

--- a/solution.py
+++ b/solution.py
@@ -24,6 +24,18 @@
 CHUNK_AT = (0, 32, 96, 160, 224)
 ORDER = (0, 2, 1, 3)
 WIDE = 1024
+
+
+FRONT = (
+    ("tstep", 0), ("tchunk", 0), ("sstart",), ("tchunk", 1), ("b2", 0), ("tstep", 1),
+    ("a2", 0), ("b2", 1), ("b3", 0), ("sstep", 0, 0), ("tchunk", 2), ("a2", 1), ("a3", 0),
+    ("tstep", 2), ("sstep", 0, 1), ("b2", 2), ("sstep", 1, 0), ("tchunk", 3), ("a3", 1),
+    ("a2", 2), ("tstep", 3), ("sstep", 1, 1), ("b2", 3), ("tchunk", 4), ("b3", 1), ("fin", 0),
+    ("b3", 2), ("sstep", 2, 0), ("sq",), ("a3", 2), ("a2", 3), ("sstep", 2, 1), ("slog", 0),
+    ("b2", 4), ("b3", 3), ("a2", 4), ("sstep", 3, 0), ("a3", 3), ("sstep", 3, 1), ("fin", 2),
+    ("b3", 4), ("a3", 4), ("slog", 1), ("fin", 1), ("fin", 3), ("slog", 2), ("fin", 4),
+)
+PIECES = ((0, 1), (2,), (3, 4))
 
 
 class Sems:
@@ -59,7 +71,7 @@
     th_ref, tg_ref, thead_hbm, sh_ref, sg_ref, shead_hbm, ids_ref,
     loss_ref, ghead_hbm, ghid_ref, ggain_ref,
     head, w, wt, h5, scaled, pa, pb, ya, xa1, xa2, xb1, xb2, yb, ssq, sqs, sqr,
-    s0, s16, f5, t4, slog, cols,
+    s0, s16, f5, t4, s4, cols,
     st_cx, st_y, st_z, ga_cx, ga_y, ga_z,
     gp, gr, perm, gh, rs, q1, q2, s2, r2, zf, zb, r3, unfolded,
     ssem, rsem,
@@ -273,25 +285,38 @@
         for cp in ex_copies(k, step, which):
             cp.start()
 
-    def ex_second(k):
-        every, rows_r, rows_l = span(k, "all"), span(k, "r"), span(k, "l")
+    def b2(k):
+        rows_r, rows_l = span(k, "r"), span(k, "l")
         ex_arrived(k, 0, "b")
         pb[1, :, rows_r] += xb1[0, :, rows_r]
         pb[3, :, rows_l] += xb1[1, :, rows_l]
         ex_send(k, 1, "b")
+
+    def a2(k):
+        every = span(k, "all")
         ex_arrived(k, 0, "a")
         pa[:, 0, every] += ya[:, every]
         ex_send(k, 1, "a")
 
-    def ex_third(k):
-        every, rows_r, rows_l = span(k, "all"), span(k, "r"), span(k, "l")
+    def b3(k):
+        every = span(k, "all")
         ex_arrived(k, 1, "b")
         pb[0, :, every] += xb2[0, :, every] + xb2[1, :, every]
         ex_send(k, 2, "b")
+
+    def a3(k):
+        rows_r, rows_l = span(k, "r"), span(k, "l")
         ex_arrived(k, 1, "a")
         pa[1, 0, rows_r] += xa1[0, rows_r]
         pa[3, 0, rows_l] += xa1[1, rows_l]
         ex_send(k, 2, "a")
+
+    def fin(k):
+        ex_arrived(k, 2)
+        for i, (_, zz) in enumerate(units(k)):
+            rows = pl.ds(CHUNK_AT[k] + 32 * i, 32)
+            t4[0, zz] = pa[0, 0, rows] + xa2[0, rows] + xa2[1, rows]
+            t4[1, zz] = pb[0, 0, rows] + yb[rows]
 
     def teacher_chunk(k):
         for i, (_, zz) in enumerate(units(k)):
@@ -325,34 +350,26 @@
             product(xo, 0)
 
     load_head.wait()
-    for s in range(4):
+
+    def tstep(s):
         ring_arrived(h5, "t", s)
         if s < 3:
             for cp in ring_copies(h5, "t", s + 1):
                 cp.start()
         for cp in sib_copies(h5, "t", s + 1):
             cp.start()
-        if s >= 2:
-            student_step(0, s - 2)
-        sib_arrived(h5, "t", s)
-        teacher_chunk(s)
-        if s == 0:
-            arrived(f5.at[1 - yh, z, c], "s_yh", 0)
-            for half in range(2):
-                for cp in half_copies(0, half):
-                    cp.start()
-            for cp in sib_copies(f5, "s", 0):
+
+    def tchunk(k):
+        sib_arrived(h5, "t", k)
+        teacher_chunk(k)
+
+    def sstart():
+        arrived(f5.at[1 - yh, z, c], "s_yh", 0)
+        for half in range(2):
+            for cp in half_copies(0, half):
                 cp.start()
-        if s >= 1:
-            ex_second(s - 1)
-        if s >= 2:
-            ex_third(s - 2)
-    student_step(1, 0)
-    sib_arrived(h5, "t", 4)
-    teacher_chunk(4)
-    wt_copy = rc(wt.at[0:SLICE], wt.at[SLICE : 2 * SLICE], "wt", 0, sibling)
-    wt_copy.start()
-    student_step(1, 1)
+        for cp in sib_copies(f5, "s", 0):
+            cp.start()
 
     def fold(*rows):
         pieces = [v[:, 128 * i : 128 * i + 128] for v in rows for i in range(4)]
@@ -365,34 +382,38 @@
     def unfold(tile, first):
         return jnp.concatenate([tile[first + i : first + i + 1, :] for i in range(4)], axis=1)
 
-    sqs[...] = fold(jnp.sum(ssq[...].reshape(TOKENS, 128).T, 0, keepdims=True))
-
     def sq_copy(j):
         return rc(sqs, sqr.at[j - 1], "sq", j, (tp, (dp + j) % 8))
 
-    for j in range(1, 8):
-        sq_copy(j).start()
-
-    ex_second(3)
-    ex_third(2)
-    student_step(2, 0)
-    ex_second(4)
-    student_step(2, 1)
-    ex_third(3)
-    student_step(3, 0)
-    ex_third(4)
-    student_step(3, 1)
-    for s in range(5):
-        sib_arrived(f5, "s", s)
-
-    for half in range(2):
-        rows = f5[half].reshape(256, D_S)
-        slog[:, half * 256 : half * 256 + 256] = jnp.dot(
-            rows, w[...], preferred_element_type=f32
-        ).T
+    wt_copy = rc(wt.at[0:SLICE], wt.at[SLICE : 2 * SLICE], "wt", 0, sibling)
+
+    def sq():
+        sqs[...] = fold(jnp.sum(ssq[...].reshape(TOKENS, 128).T, 0, keepdims=True))
+        for j in range(1, 8):
+            sq_copy(j).start()
+        wt_copy.start()
+
+    def slog(piece):
+        blocks = []
+        for s in PIECES[piece]:
+            sib_arrived(f5, "s", s)
+            blocks += [zz for _, zz in units(s)]
+        rows = jnp.concatenate([f5[:, zz].reshape(64, D_S) for zz in blocks], axis=0)
+        product = jnp.dot(rows, w[...], preferred_element_type=f32)
+        for i, zz in enumerate(blocks):
+            s4[0, zz] = product[64 * i : 64 * i + 32]
+            s4[1, zz] = product[64 * i + 32 : 64 * i + 64]
+
+    steps = {
+        "tstep": tstep, "tchunk": tchunk, "sstart": sstart, "sstep": student_step,
+        "b2": b2, "a2": a2, "b3": b3, "a3": a3, "sq": sq, "slog": slog, "fin": fin,
+    }
+    for step, *where in FRONT:
+        steps[step](*where)
+
     first = (tp * 8 + dp) * SLICE
     target_mask = ids_ref[...] == first + lax.broadcasted_iota(jnp.int32, (SLICE, TOKENS), 0)
-    student = slog[...]
+    student = s4[...].reshape(TOKENS, SLICE).T
     s_top = jnp.max(student, 0, keepdims=True)
     s_total = jnp.sum(jnp.exp(student - s_top), 0, keepdims=True)
     target = jnp.sum(jnp.where(target_mask, student, 0.0), 0, keepdims=True)
@@ -403,12 +424,6 @@
     for j in range(7):
         square_total = square_total + sqr[j]
     t_inv = unfold(lax.rsqrt(square_total / D_T + epsilon), 0)
-    for k in range(5):
-        ex_arrived(k, 2)
-        for i, (_, zz) in enumerate(units(k)):
-            rows = pl.ds(CHUNK_AT[k] + 32 * i, 32)
-            t4[0, zz] = pa[0, 0, rows] + xa2[0, rows] + xa2[1, rows]
-            t4[1, zz] = pb[0, 0, rows] + yb[rows]
     teacher = t4[...].reshape(TOKENS, SLICE).T * t_inv
 
     t_top = jnp.max(teacher, 0, keepdims=True)
@@ -502,6 +517,15 @@
             )
         for cp in q1_copies(ch):
             cp.start()
+    def head_tile(i, carry):
+        at = pl.ds(pl.multiple_of(i * 512, 512), 512)
+        features = f5[:, :, :, :, at].reshape(TOKENS, 512)
+        tile = jnp.dot(g, features, preferred_element_type=f32)
+        cols[pl.ds(i, 1), :] = jnp.sum(tile * wt[0:SLICE, at].astype(f32), 0, keepdims=True)
+        gh[at, :] = tile.astype(bf16).T
+        return carry
+
+    lax.fori_loop(0, 2, head_tile, 0)
     for ch in ORDER:
         for cp in q1_copies(ch):
             cp.wait_recv()
@@ -511,26 +535,18 @@
         for cp in q2_copies(ch):
             cp.start()
 
-    def head_tile(i, carry):
-        at = pl.ds(pl.multiple_of(i * 512, 512), 512)
-        features = f5[:, :, :, :, at].reshape(TOKENS, 512)
-        tile = jnp.dot(g, features, preferred_element_type=f32)
-        cols[pl.ds(i, 1), :] = jnp.sum(tile * wt[0:SLICE, at].astype(f32), 0, keepdims=True)
-        gh[at, :] = tile.astype(bf16).T
-        return carry
-
-    lax.fori_loop(0, 8, head_tile, 0)
-    store_head = pltpu.make_async_copy(gh, ghead_hbm, ssem.at[BASE["load"] + 2])
-    store_head.start()
-    gain = cols[...]
-    exchange(ga_cx, "ga", "cx", gain)
-
     def rs2_copy(ch, j):
         if ch < 2:
             return rc(s2.at[ch, (y + j) % 4], r2.at[ch, j - 1], "rs2", ch * 4 + j, peer("y", j))
         return rc(s2.at[ch, (x + j) % 4], r2.at[ch, j - 1], "rs2", ch * 4 + j, peer("x", j))
 
+    lax.fori_loop(2, 6, head_tile, 0)
     for ch in ORDER:
+        if ch == ORDER[2]:
+            lax.fori_loop(6, 8, head_tile, 0)
+            store_head = pltpu.make_async_copy(gh, ghead_hbm, ssem.at[BASE["load"] + 2])
+            store_head.start()
+            exchange(ga_cx, "ga", "cx", cols[...])
         for cp in q2_copies(ch):
             cp.wait_recv()
         kept = shard(ch, 0)[...].astype(f32)
@@ -651,7 +667,7 @@
         ((2, 2, 256, SLICE), f32), ((2, 2, 256, SLICE), f32), ((256, SLICE), f32),
         ((2, 8, 32, 128), f32), ((8, 128), f32), ((7, 8, 128), f32),
         ((8, 2, D_S), f32), ((16, D_S), f32), ((2, 8, 2, 16, D_S), bf16),
-        ((2, 8, 32, SLICE), f32), ((SLICE, TOKENS), f32), ((8, 512), f32),
+        ((2, 8, 32, SLICE), f32), ((2, 8, 32, SLICE), f32), ((8, 512), f32),
         ((8, 3, 8, 128), f32), ((4, 3, 8, 128), f32), ((8, 3, 8, 128), f32),
         ((8,) + row8, f32), ((4,) + row8, f32), ((8,) + row8, f32),
         ((TOKENS, SLICE), bf16), ((256, SLICE), bf16), ((TOKENS, TOKENS), bf16), ((D_S, SLICE), bf16),

time: 110 us -> 106 us (0.964)
  Pallas kernels: 109 us -> 105 us
    pallas_call x1, Pallas kernels: 106 us -> 103 us  [shards(): pl.pallas_call(kernel, out_shape=(jax.ShapeDtypeStruct((1, TOKENS), f32),...]
where the time goes in v5:
time: 106 us
  Pallas kernels  105 us (99%)
    pallas_call x1, Pallas kernels, shards(): pl.pallas_call(kernel, out_shape=(jax.ShapeDtypeStruct((1, TOKENS), f32),...  103 us
    pallas_call x1, Pallas kernels, shards(): pl.pallas_call(finish, out_shape=(jax.ShapeDtypeStruct((1, TOKENS), f32),...  2.66 us

profile of v5, /device:TPU:1, one launch (start us, length us, event | category | flops | bytes accessed | tf_op | source)
XLA Modules:
  0.0 106.1 jit_solution(2997171072045056736)
XLA Ops:
  0.6 102.8 %shard_map.102 = (f32[1,512]{1,0:T(1,128)}, bf16[4096,256]{1,0:T(8,128)(2,1)}, f32[2,4096]{1,0:T(2,128)}, f32[8,512]{1,0:T(8,128)}) custom-call(bf16[16,2048]{1,0:T(8,128)(2,1)} %th_ref.1, bf16[2048]{0:T(1024)(128)(2,1)} %tg_ref.1, bf16[2048,2048]{1,0:T(8,128)(2,1)} %thead_hbm.1, bf16[2,4096]{1,0:T(2,128)(2,1)} %sh_ref.1, bf16[4096]{0:T(1024)(128)(2,1)} %sg_ref.1, ...), custom_call_target="tpu_custom_call" | custom-call | flops 7600000000 | bytes 13000000 | tf_op jit(solution)/shard_map/pallas_call | solution.py:678
  103.4 2.7 %shard_map.103 = (f32[1,512]{1,0:T(1,128)}, bf16[2,4096]{1,0:T(2,128)(2,1)}, f32[1,4096]{1,0:T(1,128)}, bf16[4096,256]{1,0:T(8,128)(2,1)}) custom-call(f32[1,512]{1,0:T(1,128)} %get-tuple-element.12.loss_ref, f32[2,4096]{1,0:T(2,128)} %get-tuple-element.13.hidden_ref, f32[8,512]{1,0:T(8,128)} %get-tuple-element.14.gain_ref, ...), custom_call_target="tpu_custom_call" | custom-call | tf_op jit(solution)/shard_map/pallas_call | solution.py:705

commit v6 on v5

--- a/solution.py
+++ b/solution.py
@@ -78,30 +78,30 @@
 ):
     tp = lax.axis_index("tp")
     dp = lax.axis_index("dp")
-    c = tp % 2
-    z = (tp // 2) % 8
-    yh = tp // 16
-    x = dp // 2
-    yl = dp % 2
+    c = lax.rem(tp, 2)
+    z = lax.rem(lax.div(tp, 2), 8)
+    yh = lax.div(tp, 16)
+    x = lax.div(dp, 2)
+    yl = lax.rem(dp, 2)
     y = yh * 2 + yl
 
     def dev(xx, yy, zz, cc):
-        return ((yy // 2) * 16 + zz * 2 + cc, xx * 2 + yy % 2)
+        return (lax.div(yy, 2) * 16 + zz * 2 + cc, xx * 2 + lax.rem(yy, 2))
 
     def zmod(v):
-        return (v + 16) % 8
+        return lax.rem(v + 16, 8)
 
     def peer(axis, j):
         if axis == "c":
-            return dev(x, y, z, (c + j) % 2)
+            return dev(x, y, z, lax.rem(c + j, 2))
         if axis == "x":
-            return dev((x + j) % 4, y, z, c)
+            return dev(lax.rem(x + j, 4), y, z, c)
         if axis == "y":
-            return dev(x, (y + j) % 4, z, c)
+            return dev(x, lax.rem(y + j, 4), z, c)
         if axis == "cx":
-            at = (x * 2 + c + j) % 8
-            return dev(at // 2, y, z, at % 2)
-        return dev(x, y, (z + j) % 8, c)
+            at = lax.rem(x * 2 + c + j, 8)
+            return dev(lax.div(at, 2), y, z, lax.rem(at, 2))
+        return dev(x, y, lax.rem(z + j, 8), c)
 
     size = {"cx": 8, "y": 4, "z": 8}
     mine = {"cx": x * 2 + c, "y": y, "z": z}
@@ -216,7 +216,7 @@
     yh_copy(h5, "t").start()
 
     def s0_copy(j):
-        return rc(s0.at[dp], s0.at[dp], "s0", j, (tp, (dp + j) % 8))
+        return rc(s0.at[dp], s0.at[dp], "s0", j, (tp, lax.rem(dp + j, 8)))
 
     for j in range(1, 8):
         s0_copy(j).start()
@@ -236,7 +236,7 @@
         cp.start()
 
     for j in range(1, 8):
-        arrived(s0.at[(dp + 8 - j) % 8], "s0", j)
+        arrived(s0.at[lax.rem(dp + 8 - j, 8)], "s0", j)
     for d in range(8):
         s16[2 * d : 2 * d + 2, :] = s0[d]
     wide = s16[...]
@@ -332,7 +332,7 @@
         m = CHUNK_ROWS[k]
 
         def product(xo, yo):
-            d = ((x + xo) % 4) * 2 + (yl + yo) % 2
+            d = lax.rem(x + xo, 4) * 2 + lax.rem(yl + yo, 2)
             columns = pl.ds(pl.multiple_of(d * SLICE, SLICE), SLICE)
             both = jnp.dot(scaled[0 : 2 * m, :], head[:, columns], preferred_element_type=f32)
             pa[xo, yo, CHUNK_AT[k] : CHUNK_AT[k] + m, :] = both[0:m]
@@ -383,7 +383,7 @@
         return jnp.concatenate([tile[first + i : first + i + 1, :] for i in range(4)], axis=1)
 
     def sq_copy(j):
-        return rc(sqs, sqr.at[j - 1], "sq", j, (tp, (dp + j) % 8))
+        return rc(sqs, sqr.at[j - 1], "sq", j, (tp, lax.rem(dp + j, 8)))
 
     wt_copy = rc(wt.at[0:SLICE], wt.at[SLICE : 2 * SLICE], "wt", 0, sibling)
 
@@ -448,7 +448,7 @@
     def exchanged(buf, name, axis):
         n = size[axis]
         for j in range(1, n):
-            arrived(buf.at[(mine[axis] + n - j) % n], name + "_" + axis, j)
+            arrived(buf.at[lax.rem(mine[axis] + n - j, n)], name + "_" + axis, j)
         return [buf[i] for i in range(n)]
 
     upper = lax.broadcasted_iota(jnp.int32, (8, 128), 0) < 4
@@ -462,8 +462,33 @@
             other = other + p[2] * jnp.where(upper, factor, 1.0)
         return top, total, other
 
+    def front_left():
+        for buf, name in ((h5, "t"), (f5, "s")):
+            yh_copy(buf, name).wait_send()
+            for s in range(4):
+                copies = ring_copies(buf, name, s) if name == "t" else half_copies(s, 0) + half_copies(s, 1)
+                for cp in copies:
+                    cp.wait_send()
+            for s in range(5):
+                for cp in sib_copies(buf, name, s):
+                    cp.wait_send()
+        wt_copy.wait_send()
+
+    def exchange_left():
+        for j in range(1, 8):
+            s0_copy(j).wait_send()
+            sq_copy(j).wait_send()
+        for k in range(5):
+            for step in range(3):
+                for cp in ex_copies(k, step):
+                    cp.wait_send()
+
     for axis, buf in (("cx", st_cx), ("y", st_y), ("z", st_z)):
         exchange(buf, "st", axis, stats)
+        if axis == "cx":
+            front_left()
+        if axis == "z":
+            exchange_left()
         stats = merged(exchanged(buf, "st", axis))
 
     top, total, other = stats
@@ -482,11 +507,18 @@
     own_rows = pl.ds(pl.multiple_of(c * 256, 256), 256)
     gp_copy = rc(gp.at[other_rows], gr, "gp", 0, sibling)
     gp_copy.start()
+    first_own = [
+        jnp.dot(gp[own_rows, :], wt[0:SLICE, at : at + 512], preferred_element_type=f32)
+        for at in (ORDER[0] * WIDE, ORDER[0] * WIDE + 512)
+    ]
+    for axis, buf in (("cx", st_cx), ("y", st_y), ("z", st_z)):
+        for j in range(1, size[axis]):
+            exchange_copy(buf, "st", axis, j).wait_send()
 
     def shard(ch, o, part=slice(0, 4)):
         if ch < 2:
-            return rs.at[ch, (x + o) % 4, part]
-        return rs.at[ch, part, (y + o) % 4]
+            return rs.at[ch, lax.rem(x + o, 4), part]
+        return rs.at[ch, part, lax.rem(y + o, 4)]
 
     y_right = peer("y", 1)
     y_left = peer("y", 3)
@@ -511,7 +543,12 @@
     for ch in ORDER:
         for tile in range(2):
             at = ch * WIDE + tile * 512
-            product = jnp.dot(both_slices, wt[:, at : at + 512], preferred_element_type=f32)
+            if ch == ORDER[0]:
+                product = first_own[tile] + jnp.dot(
+                    gr[...], wt[SLICE : 2 * SLICE, at : at + 512], preferred_element_type=f32
+                )
+            else:
+                product = jnp.dot(both_slices, wt[:, at : at + 512], preferred_element_type=f32)
             rs[ch, :, :, :, tile * 512 : tile * 512 + 512] = product.astype(bf16).reshape(
                 4, 4, 16, 512
             )
@@ -537,8 +574,8 @@
 
     def rs2_copy(ch, j):
         if ch < 2:
-            return rc(s2.at[ch, (y + j) % 4], r2.at[ch, j - 1], "rs2", ch * 4 + j, peer("y", j))
-        return rc(s2.at[ch, (x + j) % 4], r2.at[ch, j - 1], "rs2", ch * 4 + j, peer("x", j))
+            return rc(s2.at[ch, lax.rem(y + j, 4)], r2.at[ch, j - 1], "rs2", ch * 4 + j, peer("y", j))
+        return rc(s2.at[ch, lax.rem(x + j, 4)], r2.at[ch, j - 1], "rs2", ch * 4 + j, peer("x", j))
 
     lax.fori_loop(2, 6, head_tile, 0)
     for ch in ORDER:
@@ -546,7 +583,7 @@
             lax.fori_loop(6, 8, head_tile, 0)
             store_head = pltpu.make_async_copy(gh, ghead_hbm, ssem.at[BASE["load"] + 2])
             store_head.start()
-            exchange(ga_cx, "ga", "cx", cols[...])
+            exchange(ga_z, "ga", "z", cols[...])
         for cp in q2_copies(ch):
             cp.wait_recv()
         kept = shard(ch, 0)[...].astype(f32)
@@ -555,8 +592,8 @@
         for j in range(1, 4):
             rs2_copy(ch, j).start()
 
-    gain = functools.reduce(jnp.add, exchanged(ga_cx, "ga", "cx"))
-    exchange(ga_y, "ga", "y", gain)
+    gain = functools.reduce(jnp.add, exchanged(ga_z, "ga", "z"))
+    exchange(ga_cx, "ga", "cx", gain)
 
     for ch in ORDER:
         for j in range(1, 4):
@@ -572,13 +609,27 @@
     zb[...] = zf[...].astype(bf16)
 
     def rs3_copy(j):
-        return rc(zb.at[(z + j) % 8], r3.at[j - 1], "rs3", j, peer("z", j))
+        return rc(zb.at[lax.rem(z + j, 8)], r3.at[j - 1], "rs3", j, peer("z", j))
 
     for j in range(1, 8):
         rs3_copy(j).start()
 
-    gain = functools.reduce(jnp.add, exchanged(ga_y, "ga", "y"))
-    exchange(ga_z, "ga", "z", gain)
+    gain = functools.reduce(jnp.add, exchanged(ga_cx, "ga", "cx"))
+    exchange(ga_y, "ga", "y", gain)
+
+    def gains_left(*axes):
+        for axis, buf in (("cx", ga_cx), ("y", ga_y), ("z", ga_z)):
+            if axis in axes:
+                for j in range(1, size[axis]):
+                    exchange_copy(buf, "ga", axis, j).wait_send()
+
+    gains_left("z", "cx")
+    gp_copy.wait_send()
+    for ch in range(4):
+        for cp in q1_copies(ch) + q2_copies(ch):
+            cp.wait_send()
+        for j in range(1, 4):
+            rs2_copy(ch, j).wait_send()
 
     own_wide = sh_ref[...].astype(f32)
     own_inv = lax.rsqrt(jnp.sum(own_wide * own_wide, -1, keepdims=True) / D_S + epsilon)
@@ -594,41 +645,16 @@
     inner = jnp.sum(grad_normed * own_normed, -1, keepdims=True) / D_S
     ghid_ref[...] = own_inv * (grad_normed - own_normed * inner)
 
-    gain = functools.reduce(jnp.add, exchanged(ga_z, "ga", "z"))
+    gain = functools.reduce(jnp.add, exchanged(ga_y, "ga", "y"))
     row = lax.broadcasted_iota(jnp.int32, (8, 512), 0)
     gain_rows = jnp.ones((8, 512), f32)
     for i in range(8):
         gain_rows = jnp.where(row == i, gain_row[:, 512 * i : 512 * i + 512], gain_rows)
     ggain_ref[...] = gain / gain_rows
 
-    for buf, name in ((h5, "t"), (f5, "s")):
-        yh_copy(buf, name).wait_send()
-        for s in range(4):
-            copies = ring_copies(buf, name, s) if name == "t" else half_copies(s, 0) + half_copies(s, 1)
-            for cp in copies:
-                cp.wait_send()
-        for s in range(5):
-            for cp in sib_copies(buf, name, s):
-                cp.wait_send()
+    gains_left("y")
     for j in range(1, 8):
-        s0_copy(j).wait_send()
-        sq_copy(j).wait_send()
         rs3_copy(j).wait_send()
-    for k in range(5):
-        for step in range(3):
-            for cp in ex_copies(k, step):
-                cp.wait_send()
-    for name, bufs in (("st", (st_cx, st_y, st_z)), ("ga", (ga_cx, ga_y, ga_z))):
-        for axis, buf in zip(("cx", "y", "z"), bufs):
-            for j in range(1, size[axis]):
-                exchange_copy(buf, name, axis, j).wait_send()
-    for ch in range(4):
-        for cp in q1_copies(ch) + q2_copies(ch):
-            cp.wait_send()
-        for j in range(1, 4):
-            rs2_copy(ch, j).wait_send()
-    wt_copy.wait_send()
-    gp_copy.wait_send()
     store_head.wait()
 
 

time: 106 us -> 106 us (level)
  no operation moved by 1% of the time
where the time goes in v6:
time: 106 us
  Pallas kernels  105 us (99%)
    pallas_call x1, Pallas kernels, shards(): pl.pallas_call(kernel, out_shape=(jax.ShapeDtypeStruct((1, TOKENS), f32),...  103 us
    pallas_call x1, Pallas kernels, shards(): pl.pallas_call(finish, out_shape=(jax.ShapeDtypeStruct((1, TOKENS), f32),...  2.66 us

profile of v6, /device:TPU:1, one launch (start us, length us, event | category | flops | bytes accessed | tf_op | source)
XLA Modules:
  0.0 106.0 jit_solution(9014566280802793807)
XLA Ops:
  0.6 102.7 %shard_map.102 = (f32[1,512]{1,0:T(1,128)}, bf16[4096,256]{1,0:T(8,128)(2,1)}, f32[2,4096]{1,0:T(2,128)}, f32[8,512]{1,0:T(8,128)}) custom-call(bf16[16,2048]{1,0:T(8,128)(2,1)} %th_ref.1, bf16[2048]{0:T(1024)(128)(2,1)} %tg_ref.1, bf16[2048,2048]{1,0:T(8,128)(2,1)} %thead_hbm.1, bf16[2,4096]{1,0:T(2,128)(2,1)} %sh_ref.1, bf16[4096]{0:T(1024)(128)(2,1)} %sg_ref.1, ...), custom_call_target="tpu_custom_call" | custom-call | flops 7600000000 | bytes 13000000 | tf_op jit(solution)/shard_map/pallas_call | solution.py:704
  103.3 2.7 %shard_map.103 = (f32[1,512]{1,0:T(1,128)}, bf16[2,4096]{1,0:T(2,128)(2,1)}, f32[1,4096]{1,0:T(1,128)}, bf16[4096,256]{1,0:T(8,128)(2,1)}) custom-call(f32[1,512]{1,0:T(1,128)} %get-tuple-element.12.loss_ref, f32[2,4096]{1,0:T(2,128)} %get-tuple-element.13.hidden_ref, f32[8,512]{1,0:T(8,128)} %get-tuple-element.14.gain_ref, ...), custom_call_target="tpu_custom_call" | custom-call | tf_op jit(solution)/shard_map/pallas_call | solution.py:731

commit v7 on v6

--- a/solution.py
+++ b/solution.py
@@ -27,13 +27,15 @@
 
 
 FRONT = (
-    ("tstep", 0), ("tchunk", 0), ("sstart",), ("tchunk", 1), ("b2", 0), ("tstep", 1),
-    ("a2", 0), ("b2", 1), ("b3", 0), ("sstep", 0, 0), ("tchunk", 2), ("a2", 1), ("a3", 0),
-    ("tstep", 2), ("sstep", 0, 1), ("b2", 2), ("sstep", 1, 0), ("tchunk", 3), ("a3", 1),
-    ("a2", 2), ("tstep", 3), ("sstep", 1, 1), ("b2", 3), ("tchunk", 4), ("b3", 1), ("fin", 0),
-    ("b3", 2), ("sstep", 2, 0), ("sq",), ("a3", 2), ("a2", 3), ("sstep", 2, 1), ("slog", 0),
-    ("b2", 4), ("b3", 3), ("a2", 4), ("sstep", 3, 0), ("a3", 3), ("sstep", 3, 1), ("fin", 2),
-    ("b3", 4), ("a3", 4), ("slog", 1), ("fin", 1), ("fin", 3), ("slog", 2), ("fin", 4),
+    ("turn",), ("th", 0, 0), ("t0",), ("th", 1, 0), ("feat",), ("th", 0, 1), ("tchunk", 0),
+    ("th", 1, 1), ("th", 2, 0), ("sstart",), ("tchunk", 1), ("th", 2, 1), ("b2", 0), ("a2", 0),
+    ("tchunk", 2), ("b2", 1), ("sstep", 0, 0), ("th", 3, 0), ("tchunk", 3), ("th", 3, 1),
+    ("sstep", 0, 1), ("b3", 0), ("a3", 0), ("b2", 2), ("a2", 1), ("sstep", 1, 0),
+    ("tchunk", 4), ("sstep", 1, 1), ("b2", 3), ("a2", 2), ("sstep", 2, 0), ("b3", 1),
+    ("a3", 1), ("a2", 3), ("sstep", 2, 1), ("b3", 2), ("fin", 0), ("b2", 4), ("slog", 0),
+    ("a3", 2), ("a2", 4), ("a3", 3), ("sstep", 3, 0), ("b3", 3), ("b3", 4), ("sstep", 3, 1),
+    ("sq",), ("fin", 1), ("a3", 4), ("slog", 1), ("fin", 2), ("fin", 3), ("slog", 2),
+    ("fin", 4),
 )
 PIECES = ((0, 1), (2,), (3, 4))
 
@@ -53,7 +55,7 @@
     base = {}
     for name, n in (
         ("load", 3),
-        ("t_yh", 1), ("t_r", 4), ("t_l", 4), ("t_s", 8),
+        ("t_yh", 1), ("t_r", 8), ("t_l", 8), ("t_s", 8),
         ("s_yh", 1), ("s_r", 8), ("s_l", 8), ("s_s", 8),
         ("s0", 8), ("ex", 50), ("sq", 8),
         ("st_cx", 8), ("st_y", 4), ("st_z", 8),
@@ -158,43 +160,33 @@
         own_block = buf.at[yh, z, c]
         return rc(own_block, own_block, name + "_yh", 0, yh_peer if name == "t" else y_outer)
 
-    def ring_copies(buf, name, s):
-        if s < 3:
-            r, l = buf.at[:, zmod(z - s), c], buf.at[:, zmod(z + s), c]
-        else:
-            r, l = buf.at[0, zmod(z - s), c], buf.at[1, zmod(z + s), c]
-        return rc(r, r, name + "_r", s, right), rc(l, l, name + "_l", s, left)
-
-    def ring_arrived(buf, name, s):
-        if s < 3:
-            r, l = buf.at[:, zmod(z - 1 - s), c], buf.at[:, zmod(z + 1 + s), c]
-        else:
-            r, l = buf.at[0, zmod(z + 4), c], buf.at[1, zmod(z + 4), c]
-        arrived(r, name + "_r", s)
-        arrived(l, name + "_l", s)
-
-    def half_copies(s, half):
-        r, l = f5.at[half, zmod(z - s), c], f5.at[half, zmod(z + s), c]
+    def half_copies(buf, name, s, half):
+        of = yh if half == 0 else 1 - yh
+        r, l = buf.at[of, zmod(z - s), c], buf.at[of, zmod(z + s), c]
         copies = []
         if s < 3 or half == 0:
-            copies.append(rc(r, r, "s_r", 2 * s + half, right))
+            copies.append(rc(r, r, name + "_r", 2 * s + half, right))
         if s < 3 or half == 1:
-            copies.append(rc(l, l, "s_l", 2 * s + half, left))
+            copies.append(rc(l, l, name + "_l", 2 * s + half, left))
         return copies
 
-    def half_arrived(s, half):
+    def half_arrived(buf, name, s, half):
+        of = yh if half == 0 else 1 - yh
         if s < 3 or half == 0:
-            arrived(f5.at[half, zmod(z - 1 - s), c], "s_r", 2 * s + half)
+            arrived(buf.at[of, zmod(z - 1 - s), c], name + "_r", 2 * s + half)
         if s < 3 or half == 1:
-            arrived(f5.at[half, zmod(z + 1 + s), c], "s_l", 2 * s + half)
-
-    def student_step(s, half):
-        half_arrived(s, half)
+            arrived(buf.at[of, zmod(z + 1 + s), c], name + "_l", 2 * s + half)
+
+    def ring_send(buf, name, s, half):
+        for cp in half_copies(buf, name, s, half):
+            cp.start()
+
+    def ring_step(buf, name, s, half):
+        half_arrived(buf, name, s, half)
         if s < 3:
-            for cp in half_copies(s + 1, half):
-                cp.start()
+            ring_send(buf, name, s + 1, half)
         if half == 1:
-            for cp in sib_copies(f5, "s", s + 1):
+            for cp in sib_copies(buf, name, s + 1):
                 cp.start()
 
     def units(s):
@@ -214,6 +206,7 @@
             arrived(buf.at[:, zz, 1 - c], name + "_s", k)
 
     yh_copy(h5, "t").start()
+    ring_send(h5, "t", 0, 0)
 
     def s0_copy(j):
         return rc(s0.at[dp], s0.at[dp], "s0", j, (tp, lax.rem(dp + j, 8)))
@@ -221,29 +214,33 @@
     for j in range(1, 8):
         s0_copy(j).start()
 
-    load_w.wait()
-
-    def turn(i, carry):
-        at = pl.ds(pl.multiple_of(i * 512, 512), 512)
-        wt[0:SLICE, at] = w[at, :].T
-        return carry
-
-    lax.fori_loop(0, 8, turn, 0)
-    arrived(h5.at[1 - yh, z, c], "t_yh", 0)
-    for cp in ring_copies(h5, "t", 0):
-        cp.start()
-    for cp in sib_copies(h5, "t", 0):
-        cp.start()
-
-    for j in range(1, 8):
-        arrived(s0.at[lax.rem(dp + 8 - j, 8)], "s0", j)
-    for d in range(8):
-        s16[2 * d : 2 * d + 2, :] = s0[d]
-    wide = s16[...]
-    inv16 = lax.rsqrt(jnp.sum(wide * wide, -1, keepdims=True) / D_S + epsilon)
+    def turn():
+        load_w.wait()
+
+        def tile(i, carry):
+            at = pl.ds(pl.multiple_of(i * 512, 512), 512)
+            wt[0:SLICE, at] = w[at, :].T
+            return carry
+
+        lax.fori_loop(0, 8, tile, 0)
+
+    def t0():
+        arrived(h5.at[1 - yh, z, c], "t_yh", 0)
+        ring_send(h5, "t", 0, 1)
+        for cp in sib_copies(h5, "t", 0):
+            cp.start()
+
     gain_row = sg_ref[...].astype(f32).reshape(1, D_S)
-    f5[yh, z, c] = (wide * inv16 * gain_row).astype(bf16)
-    yh_copy(f5, "s").start()
+
+    def feat():
+        for j in range(1, 8):
+            arrived(s0.at[lax.rem(dp + 8 - j, 8)], "s0", j)
+        for d in range(8):
+            s16[2 * d : 2 * d + 2, :] = s0[d]
+        wide = s16[...]
+        inv16 = lax.rsqrt(jnp.sum(wide * wide, -1, keepdims=True) / D_S + epsilon)
+        f5[yh, z, c] = (wide * inv16 * gain_row).astype(bf16)
+        yh_copy(f5, "s").start()
 
     tg = tg_ref[...].astype(f32).reshape(1, 2048)
 
@@ -349,25 +346,16 @@
         for xo in (1, 3, 0):
             product(xo, 0)
 
-    load_head.wait()
-
-    def tstep(s):
-        ring_arrived(h5, "t", s)
-        if s < 3:
-            for cp in ring_copies(h5, "t", s + 1):
-                cp.start()
-        for cp in sib_copies(h5, "t", s + 1):
-            cp.start()
-
     def tchunk(k):
+        if k == 0:
+            load_head.wait()
         sib_arrived(h5, "t", k)
         teacher_chunk(k)
 
     def sstart():
         arrived(f5.at[1 - yh, z, c], "s_yh", 0)
-        for half in range(2):
-            for cp in half_copies(0, half):
-                cp.start()
+        ring_send(f5, "s", 0, 0)
+        ring_send(f5, "s", 0, 1)
         for cp in sib_copies(f5, "s", 0):
             cp.start()
 
@@ -405,7 +393,8 @@
             s4[1, zz] = product[64 * i + 32 : 64 * i + 64]
 
     steps = {
-        "tstep": tstep, "tchunk": tchunk, "sstart": sstart, "sstep": student_step,
+        "turn": turn, "t0": t0, "feat": feat, "tchunk": tchunk, "sstart": sstart,
+        "th": functools.partial(ring_step, h5, "t"), "sstep": functools.partial(ring_step, f5, "s"),
         "b2": b2, "a2": a2, "b3": b3, "a3": a3, "sq": sq, "slog": slog, "fin": fin,
     }
     for step, *where in FRONT:
@@ -466,8 +455,7 @@
         for buf, name in ((h5, "t"), (f5, "s")):
             yh_copy(buf, name).wait_send()
             for s in range(4):
-                copies = ring_copies(buf, name, s) if name == "t" else half_copies(s, 0) + half_copies(s, 1)
-                for cp in copies:
+                for cp in half_copies(buf, name, s, 0) + half_copies(buf, name, s, 1):
                     cp.wait_send()
             for s in range(5):
                 for cp in sib_copies(buf, name, s):

time: 106 us -> 103 us (0.972)
  Pallas kernels: 105 us -> 102 us
    pallas_call x1, Pallas kernels: 103 us -> 99.7 us  [shards(): pl.pallas_call(kernel, out_shape=(jax.ShapeDtypeStruct((1, TOKENS), f32),...]
where the time goes in v7:
time: 103 us
  Pallas kernels  102 us (99%)
    pallas_call x1, Pallas kernels, shards(): pl.pallas_call(kernel, out_shape=(jax.ShapeDtypeStruct((1, TOKENS), f32),...  99.7 us
    pallas_call x1, Pallas kernels, shards(): pl.pallas_call(finish, out_shape=(jax.ShapeDtypeStruct((1, TOKENS), f32),...  2.66 us

profile of v7, /device:TPU:1, one launch (start us, length us, event | category | flops | bytes accessed | tf_op | source)
XLA Modules:
  0.0 103.0 jit_solution(807597979158023764)
XLA Ops:
  0.6 99.7 %shard_map.102 = (f32[1,512]{1,0:T(1,128)}, bf16[4096,256]{1,0:T(8,128)(2,1)}, f32[2,4096]{1,0:T(2,128)}, f32[8,512]{1,0:T(8,128)}) custom-call(bf16[16,2048]{1,0:T(8,128)(2,1)} %th_ref.1, bf16[2048]{0:T(1024)(128)(2,1)} %tg_ref.1, bf16[2048,2048]{1,0:T(8,128)(2,1)} %thead_hbm.1, bf16[2,4096]{1,0:T(2,128)(2,1)} %sh_ref.1, bf16[4096]{0:T(1024)(128)(2,1)} %sg_ref.1, ...), custom_call_target="tpu_custom_call" | custom-call | flops 7600000000 | bytes 13000000 | tf_op jit(solution)/shard_map/pallas_call | solution.py:692
  100.3 2.7 %shard_map.103 = (f32[1,512]{1,0:T(1,128)}, bf16[2,4096]{1,0:T(2,128)(2,1)}, f32[1,4096]{1,0:T(1,128)}, bf16[4096,256]{1,0:T(8,128)(2,1)}) custom-call(f32[1,512]{1,0:T(1,128)} %get-tuple-element.12.loss_ref, f32[2,4096]{1,0:T(2,128)} %get-tuple-element.13.hidden_ref, f32[8,512]{1,0:T(8,128)} %get-tuple-element.14.gain_ref, ...), custom_call_target="tpu_custom_call" | custom-call | tf_op jit(solution)/shard_map/pallas_call | solution.py:719

commit v8 on v7

--- a/solution.py
+++ b/solution.py
@@ -60,7 +60,7 @@
         ("s0", 8), ("ex", 50), ("sq", 8),
         ("st_cx", 8), ("st_y", 4), ("st_z", 8),
         ("ga_cx", 8), ("ga_y", 4), ("ga_z", 8),
-        ("wt", 1), ("gp", 1), ("q1", 8), ("q2", 8), ("rs2", 16), ("rs3", 8),
+        ("wt", 1), ("gp", 1), ("q1", 8), ("q2", 8), ("q3", 8), ("rs2", 16), ("rs3", 8),
     ):
         base[name] = s.take(n)
     return base, s.count
@@ -489,12 +489,12 @@
     onehot = target_mask.astype(f32)
     g = (loss_scale * (s_prob - t_prob + hard_weight * (s_prob - onehot))).astype(bf16)
 
-    gp[...] = jnp.dot(g, perm[...], preferred_element_type=f32).astype(bf16).T
-
     other_rows = pl.ds(pl.multiple_of((1 - c) * 256, 256), 256)
     own_rows = pl.ds(pl.multiple_of(c * 256, 256), 256)
     gp_copy = rc(gp.at[other_rows], gr, "gp", 0, sibling)
+    gp[other_rows, :] = jnp.dot(g, perm[:, other_rows], preferred_element_type=f32).astype(bf16).T
     gp_copy.start()
+    gp[own_rows, :] = jnp.dot(g, perm[:, own_rows], preferred_element_type=f32).astype(bf16).T
     first_own = [
         jnp.dot(gp[own_rows, :], wt[0:SLICE, at : at + 512], preferred_element_type=f32)
         for at in (ORDER[0] * WIDE, ORDER[0] * WIDE + 512)
@@ -520,9 +520,18 @@
 
     def q2_copies(ch):
         r, l = (x_right, x_left) if ch < 2 else (y_right, y_left)
+        low, high = slice(0, 2), slice(2, 4)
         return (
-            rc(shard(ch, 1), q2.at[ch, 0], "q2", ch * 2, r),
-            rc(shard(ch, 3), q2.at[ch, 1], "q2", ch * 2 + 1, l),
+            rc(shard(ch, 1, low), q2.at[ch, 0, low], "q2", ch * 2, r),
+            rc(shard(ch, 3, high), q2.at[ch, 1, high], "q2", ch * 2 + 1, l),
+        )
+
+    def q3_copies(ch):
+        r, l = (x_right, x_left) if ch < 2 else (y_right, y_left)
+        low, high = slice(0, 2), slice(2, 4)
+        return (
+            rc(shard(ch, 1, high), q2.at[ch, 0, high], "q3", ch * 2, r),
+            rc(shard(ch, 3, low), q2.at[ch, 1, low], "q3", ch * 2 + 1, l),
         )
 
     arrived(wt.at[SLICE : 2 * SLICE], "wt", 0)
@@ -542,6 +551,8 @@
             )
         for cp in q1_copies(ch):
             cp.start()
+        for cp in q3_copies(ch):
+            cp.start()
     def head_tile(i, carry):
         at = pl.ds(pl.multiple_of(i * 512, 512), 512)
         features = f5[:, :, :, :, at].reshape(TOKENS, 512)
@@ -572,7 +583,7 @@
             store_head = pltpu.make_async_copy(gh, ghead_hbm, ssem.at[BASE["load"] + 2])
             store_head.start()
             exchange(ga_z, "ga", "z", cols[...])
-        for cp in q2_copies(ch):
+        for cp in q2_copies(ch) + q3_copies(ch):
             cp.wait_recv()
         kept = shard(ch, 0)[...].astype(f32)
         total = kept + (q2[ch, 0].astype(f32) + q2[ch, 1].astype(f32))
@@ -614,7 +625,7 @@
     gains_left("z", "cx")
     gp_copy.wait_send()
     for ch in range(4):
-        for cp in q1_copies(ch) + q2_copies(ch):
+        for cp in q1_copies(ch) + q2_copies(ch) + q3_copies(ch):
             cp.wait_send()
         for j in range(1, 4):
             rs2_copy(ch, j).wait_send()

time: 103 us -> 103 us (level)
  no operation moved by 1% of the time
where the time goes in v8:
time: 103 us
  Pallas kernels  103 us (100%)
    pallas_call x1, Pallas kernels, shards(): pl.pallas_call(kernel, out_shape=(jax.ShapeDtypeStruct((1, TOKENS), f32),...  100 us
    pallas_call x1, Pallas kernels, shards(): pl.pallas_call(finish, out_shape=(jax.ShapeDtypeStruct((1, TOKENS), f32),...  2.66 us

profile of v8, /device:TPU:1, one launch (start us, length us, event | category | flops | bytes accessed | tf_op | source)
XLA Modules:
  0.0 103.3 jit_solution(2245807804112717951)
XLA Ops:
  0.6 100.0 %shard_map.102 = (f32[1,512]{1,0:T(1,128)}, bf16[4096,256]{1,0:T(8,128)(2,1)}, f32[2,4096]{1,0:T(2,128)}, f32[8,512]{1,0:T(8,128)}) custom-call(bf16[16,2048]{1,0:T(8,128)(2,1)} %th_ref.1, bf16[2048]{0:T(1024)(128)(2,1)} %tg_ref.1, bf16[2048,2048]{1,0:T(8,128)(2,1)} %thead_hbm.1, bf16[2,4096]{1,0:T(2,128)(2,1)} %sh_ref.1, bf16[4096]{0:T(1024)(128)(2,1)} %sg_ref.1, ...), custom_call_target="tpu_custom_call" | custom-call | flops 7600000000 | bytes 13000000 | tf_op jit(solution)/shard_map/pallas_call | solution.py:703
  100.6 2.7 %shard_map.103 = (f32[1,512]{1,0:T(1,128)}, bf16[2,4096]{1,0:T(2,128)(2,1)}, f32[1,4096]{1,0:T(1,128)}, bf16[4096,256]{1,0:T(8,128)(2,1)}) custom-call(f32[1,512]{1,0:T(1,128)} %get-tuple-element.12.loss_ref, f32[2,4096]{1,0:T(2,128)} %get-tuple-element.13.hidden_ref, f32[8,512]{1,0:T(8,128)} %get-tuple-element.14.gain_ref, ...), custom_call_target="tpu_custom_call" | custom-call | tf_op jit(solution)/shard_map/pallas_call | solution.py:730

commit v9 on v7

--- a/solution.py
+++ b/solution.py
@@ -550,7 +550,7 @@
         gh[at, :] = tile.astype(bf16).T
         return carry
 
-    lax.fori_loop(0, 2, head_tile, 0)
+    lax.fori_loop(0, 4, head_tile, 0)
     for ch in ORDER:
         for cp in q1_copies(ch):
             cp.wait_recv()
@@ -565,13 +565,11 @@
             return rc(s2.at[ch, lax.rem(y + j, 4)], r2.at[ch, j - 1], "rs2", ch * 4 + j, peer("y", j))
         return rc(s2.at[ch, lax.rem(x + j, 4)], r2.at[ch, j - 1], "rs2", ch * 4 + j, peer("x", j))
 
-    lax.fori_loop(2, 6, head_tile, 0)
+    lax.fori_loop(4, 8, head_tile, 0)
+    store_head = pltpu.make_async_copy(gh, ghead_hbm, ssem.at[BASE["load"] + 2])
+    store_head.start()
+    exchange(ga_z, "ga", "z", cols[...])
     for ch in ORDER:
-        if ch == ORDER[2]:
-            lax.fori_loop(6, 8, head_tile, 0)
-            store_head = pltpu.make_async_copy(gh, ghead_hbm, ssem.at[BASE["load"] + 2])
-            store_head.start()
-            exchange(ga_z, "ga", "z", cols[...])
         for cp in q2_copies(ch):
             cp.wait_recv()
         kept = shard(ch, 0)[...].astype(f32)

time: 103 us -> 102 us (level)
    pallas_call x1, Pallas kernels: 99.7 us -> 98.2 us  [shards(): pl.pallas_call(kernel, out_shape=(jax.ShapeDtypeStruct((1, TOKENS), f32),...]
where the time goes in v9:
time: 102 us
  Pallas kernels  101 us (99%)
    pallas_call x1, Pallas kernels, shards(): pl.pallas_call(kernel, out_shape=(jax.ShapeDtypeStruct((1, TOKENS), f32),...  98.2 us
    pallas_call x1, Pallas kernels, shards(): pl.pallas_call(finish, out_shape=(jax.ShapeDtypeStruct((1, TOKENS), f32),...  2.66 us

profile of v9, /device:TPU:1, one launch (start us, length us, event | category | flops | bytes accessed | tf_op | source)
XLA Modules:
  0.0 101.5 jit_solution(11435044120462405023)
XLA Ops:
  0.6 98.2 %shard_map.102 = (f32[1,512]{1,0:T(1,128)}, bf16[4096,256]{1,0:T(8,128)(2,1)}, f32[2,4096]{1,0:T(2,128)}, f32[8,512]{1,0:T(8,128)}) custom-call(bf16[16,2048]{1,0:T(8,128)(2,1)} %th_ref.1, bf16[2048]{0:T(1024)(128)(2,1)} %tg_ref.1, bf16[2048,2048]{1,0:T(8,128)(2,1)} %thead_hbm.1, bf16[2,4096]{1,0:T(2,128)(2,1)} %sh_ref.1, bf16[4096]{0:T(1024)(128)(2,1)} %sg_ref.1, ...), custom_call_target="tpu_custom_call" | custom-call | flops 7600000000 | bytes 13000000 | tf_op jit(solution)/shard_map/pallas_call | solution.py:690
  98.9 2.7 %shard_map.103 = (f32[1,512]{1,0:T(1,128)}, bf16[2,4096]{1,0:T(2,128)(2,1)}, f32[1,4096]{1,0:T(1,128)}, bf16[4096,256]{1,0:T(8,128)(2,1)}) custom-call(f32[1,512]{1,0:T(1,128)} %get-tuple-element.12.loss_ref, f32[2,4096]{1,0:T(2,128)} %get-tuple-element.13.hidden_ref, f32[8,512]{1,0:T(8,128)} %get-tuple-element.14.gain_ref, ...), custom_call_target="tpu_custom_call" | custom-call | tf_op jit(solution)/shard_map/pallas_call | solution.py:717
